TPU v7x, 256 devices: a whole 4x4x8 slice. The times are simulated.
256 devices in a mesh: fsdp: 32 (over y, z), gen: 4 (over x_lo, core), tp: 2 (over x_hi).
Axes of the slice: x: 4 (x_hi: 2, x_lo: 2; x = x_hi * 2 + x_lo), y: 4, z: 8, core: 2. Of those that a mesh axis runs over, the one named last changes fastest.
Arguments:
- master_weight: float32 [2, 5120, 1024], P(None, ('fsdp', 'gen'), 'tp'), may hold values from -0.078125 to 0.078125
- gradient: float32 [2, 5120, 1024], P(None, ('fsdp', 'gen'), 'tp'), may hold values from -6 to 6
- first_moment: float32 [2, 5120, 1024], P(None, ('fsdp', 'gen'), 'tp'), may hold values from -1.8 to 1.8
- second_moment: float32 [2, 5120, 1024], P(None, ('fsdp', 'gen'), 'tp'), may hold values from 0.1 to 4
- new_inputs: bfloat16 [4096, 4, 5120], P(('fsdp', 'gen')), may hold values from -6 to 6
- queries: bfloat16 [4096, 4, 64, 128], P(('fsdp', 'gen'), None, 'tp'), may hold values from -41 to 41
- cache_keys: bfloat16 [4096, 128, 8, 128], P(('fsdp', 'gen'), None, 'tp'), may hold values from -6 to 6
- cache_values: bfloat16 [4096, 128, 8, 128], P(('fsdp', 'gen'), None, 'tp'), may hold values from -6 to 6
- prefix_lengths: int32 [4096], P(('fsdp', 'gen')), may hold values from 2 to 128
- rollout_lengths: int32 [4096], P(('fsdp', 'gen')), may hold values from 1 to 4
- destinations: int32 [4096], P(('fsdp', 'gen')), may hold values from 0 to 31, as said below
Outputs:
- new_master: float32 [2, 5120, 1024], P(None, ('fsdp', 'gen'), 'tp')
- new_first: float32 [2, 5120, 1024], P(None, ('fsdp', 'gen'), 'tp')
- new_second: float32 [2, 5120, 1024], P(None, ('fsdp', 'gen'), 'tp')
- fresh_kv: bfloat16 [4096, 4, 2, 8, 128], P(('fsdp', 'gen'), None, None, 'tp')
- returned_rows: bfloat16 [32, 4, 32, 2, 4, 8192], P('fsdp', 'gen', None, None, None, 'tp')
Inputs may be any that keep to these rules, and one draw needn't show every extreme that they name: `destinations`: within the 32 rollouts of one group, no trainer shard is named more than 2 times; in every group one shard is named exactly 2 times.
All inputs are finite; a program needn't handle non-finite values.
Results may differ from a plain program's by a relative error of at most 0.0053.
Values may be sent and summed in bfloat16 or wider, within the bound.
No kernel may reach another device: no remote copies, remote signals or barrier semaphores. Data moves between devices by JAX's collectives and lax.ppermute only.
A program may use at most 128 MiB of HBM per device.

v0:
```python
import jax
import jax.numpy as jnp
from jax import lax
from jax.sharding import PartitionSpec as P

beta_one = 0.9
beta_two = 0.95
adam_eps = 1e-08
learn_rate = 0.002
weight_decay = 0.1
adam_step = 10.0
rope_theta = 1000000.0
norm_eps = 1e-06
masked_score = -1e30


def adam_update(master_weight, gradient, first_moment, second_moment):
    first_next = beta_one * first_moment + (1.0 - beta_one) * gradient
    second_next = beta_two * second_moment + (1.0 - beta_two) * gradient * gradient
    first_hat = first_next / (1.0 - beta_one**adam_step)
    second_hat = second_next / (1.0 - beta_two**adam_step)
    master_next = master_weight - learn_rate * (
        first_hat / (jnp.sqrt(second_hat) + adam_eps) + weight_decay * master_weight
    )
    return (master_next, first_next, second_next)


def rotate(vectors, positions):
    half_size = vectors.shape[-1] // 2
    exponent = -2.0 * jnp.arange(half_size).astype(jnp.float32) / vectors.shape[-1]
    inverse_freq = jnp.power(jnp.float32(rope_theta), exponent)
    angle = positions.astype(jnp.float32)[..., None] * inverse_freq
    cosine = jnp.cos(angle)
    sine = jnp.sin(angle)
    first_half = vectors[..., :half_size]
    second_half = vectors[..., half_size:]
    return jnp.concatenate(
        [first_half * cosine - second_half * sine, second_half * cosine + first_half * sine],
        axis=-1,
    )


def key_norm(raw_keys):
    return raw_keys / jnp.sqrt(jnp.mean(raw_keys * raw_keys, axis=-1, keepdims=True) + norm_eps)


def row_adder(flat_inputs, piece):
    key_part = jnp.dot(flat_inputs, piece[0], preferred_element_type=jnp.float32)
    value_part = jnp.dot(flat_inputs, piece[1], preferred_element_type=jnp.float32)
    return (key_part, value_part)


def on_device(
    master_weight,
    gradient,
    first_moment,
    second_moment,
    new_inputs,
    queries,
    cache_keys,
    cache_values,
    prefix_lengths,
    rollout_lengths,
    destinations,
):
    new_master, new_first, new_second = adam_update(
        master_weight, gradient, first_moment, second_moment
    )
    weight_bf = new_master.astype(jnp.bfloat16)
    roll_count = new_inputs.shape[0]
    step_count = new_inputs.shape[1]
    head_size = cache_keys.shape[3]
    local_heads = cache_keys.shape[2]
    cache_slots = cache_keys.shape[1]
    flat_inputs = new_inputs.reshape(roll_count * step_count, -1)
    raw_keys, raw_values = row_adder(
        flat_inputs, lax.all_gather(weight_bf, ("fsdp", "gen"), axis=1, tiled=True)
    )
    raw_keys = raw_keys.reshape(roll_count, step_count, local_heads, head_size)
    raw_values = raw_values.reshape(roll_count, step_count, local_heads, head_size)
    positions = prefix_lengths[:, None] + jnp.arange(step_count, dtype=jnp.int32)[None, :]
    fresh_keys = rotate(key_norm(raw_keys), positions[:, :, None]).astype(jnp.bfloat16)
    fresh_values = raw_values.astype(jnp.bfloat16)
    fresh_kv = jnp.stack([fresh_keys, fresh_values], axis=2)
    score_scale = head_size ** (-0.5)
    grouped = queries.reshape(roll_count, step_count, local_heads, -1, head_size)
    old_scores = (
        jnp.einsum("rsgqh,rcgh->rgqsc", grouped, cache_keys, preferred_element_type=jnp.float32)
        * score_scale
    )
    new_scores = (
        jnp.einsum("rsgqh,rtgh->rgqst", grouped, fresh_keys, preferred_element_type=jnp.float32)
        * score_scale
    )
    old_mask = jnp.arange(cache_slots)[None, :] < prefix_lengths[:, None]
    new_mask = jnp.arange(step_count)[None, :] <= jnp.arange(step_count)[:, None]
    old_scores = jnp.where(old_mask[:, None, None, None, :], old_scores, masked_score)
    new_scores = jnp.where(new_mask[None, None, None], new_scores, masked_score)
    row_max = jnp.maximum(jnp.max(old_scores, axis=-1), jnp.max(new_scores, axis=-1))
    old_exp = jnp.exp(old_scores - row_max[..., None])
    new_exp = jnp.exp(new_scores - row_max[..., None])
    row_total = jnp.sum(old_exp, axis=-1) + jnp.sum(new_exp, axis=-1)
    old_weight = (old_exp / row_total[..., None]).astype(jnp.bfloat16)
    new_weight = (new_exp / row_total[..., None]).astype(jnp.bfloat16)
    mixed = jnp.einsum(
        "rgqsc,rcgh->rsgqh", old_weight, cache_values, preferred_element_type=jnp.float32
    )
    mixed = mixed + jnp.einsum(
        "rgqst,rtgh->rsgqh", new_weight, fresh_values, preferred_element_type=jnp.float32
    )
    attention = mixed.astype(jnp.bfloat16).reshape(roll_count, step_count, -1)
    kept = jnp.arange(step_count)[None, :] < rollout_lengths[:, None]
    token_rows = jnp.where(kept[:, :, None], attention, jnp.zeros_like(attention))
    shard_count = lax.axis_size("fsdp")
    slot_most = max(2, 2 * roll_count // shard_count)
    same_dest = destinations[:, None] == destinations[None, :]
    earlier = jnp.arange(roll_count)[None, :] < jnp.arange(roll_count)[:, None]
    slot_rank = jnp.sum((same_dest & earlier).astype(jnp.int32), axis=1)
    dest_match = destinations[None, None, :] == jnp.arange(shard_count)[:, None, None]
    rank_match = slot_rank[None, None, :] == jnp.arange(slot_most)[None, :, None]
    selector = (dest_match & rank_match).astype(jnp.bfloat16)
    outgoing = jnp.einsum(
        "djr,rsw->djsw", selector, token_rows, preferred_element_type=jnp.float32
    ).astype(jnp.bfloat16)
    incoming = lax.all_to_all(outgoing, "fsdp", split_axis=0, concat_axis=0, tiled=True)
    returned_rows = incoming[None, None]
    return (new_master, new_first, new_second, fresh_kv, returned_rows)


def solution(mesh):
    in_specs = (
        P(None, ("fsdp", "gen"), "tp"),
        P(None, ("fsdp", "gen"), "tp"),
        P(None, ("fsdp", "gen"), "tp"),
        P(None, ("fsdp", "gen"), "tp"),
        P(("fsdp", "gen"), None, None),
        P(("fsdp", "gen"), None, "tp", None),
        P(("fsdp", "gen"), None, "tp", None),
        P(("fsdp", "gen"), None, "tp", None),
        P(("fsdp", "gen")),
        P(("fsdp", "gen")),
        P(("fsdp", "gen")),
    )
    out_specs = (
        P(None, ("fsdp", "gen"), "tp"),
        P(None, ("fsdp", "gen"), "tp"),
        P(None, ("fsdp", "gen"), "tp"),
        P(("fsdp", "gen"), None, None, "tp", None),
        P("fsdp", "gen", None, None, None, "tp"),
    )
    return jax.shard_map(
        on_device, mesh=mesh, in_specs=in_specs, out_specs=out_specs, check_vma=False
    )
```

profile of v0, /device:TPU:1, one launch (start us, length us, event | category | flops | bytes accessed | tf_op | source)
XLA Modules:
  0.0 337.7 jit_solution(8007871782256621547)
XLA Ops:
  7.3 2.2 fusion.44
  9.5 1.2 reshape.224
  10.7 0.5 iota_compare_fusion.3
  11.4 0.5 iota_compare_fusion.4
  12.6 1.2 multiply_cosine_fusion
  13.8 5.3 %bitcast_reduce_fusion = (f32[32,4,8,4]{2,3,1,0:T(4,128)}, f32[32,4,128,4,8]{2,4,3,1,0:T(8,128)S(1)}) fusion(pred[32,128]{1,0:T(8,128)(4,1)S(1)} %iota_compare_fusion, bf16[32,128,4,128,1]{3,2,1,0,4:T(4,128)(2,1)} %bitcast.74, bf16[32,4,32,128]{3,2,1,0:T(8,128)(2,1)S(1)} %copy-done), kind=kOutput, calls=%fused_computation.12 | convolution fusion | flops 135786496 | bytes 7360512 | tf_op jit(solution)/shard_map/rsgqh,rcgh->rgqsc/dot_general | solution.py:88
  19.1 218.3 %all-gather.2.cloned.1.call-done = bf16[2,5120,512]{2,1,0:T(8,128)(2,1)} async-done(((bf16[2,40,512]{2,1,0:T(8,128)(2,1)}), bf16[2,5120,512]{2,1,0:T(8,128)(2,1)}) %all-gather.2.cloned.1.call-update) | async-done | bytes 10485776 | tf_op jit(solution)/shard_map/all_gather | solution.py:77
  237.4 4.4 %fusion.15 = bf16[128,512]{0,1:T(8,128)(2,1)S(1)} fusion(bf16[128,5120]{1,0:T(8,128)(2,1)} %reshape.224, bf16[2,5120,512]{2,1,0:T(8,128)(2,1)} %all-gather.2.cloned.1.call-done), kind=kOutput, calls=%fused_computation.22 | convolution fusion | flops 671154176 | bytes 6684672 | tf_op jit(solution)/shard_map/dot_general | solution.py:49
  242.0 4.4 %fusion.13 = f32[128,512]{0,1:T(8,128)S(1)} fusion(bf16[128,5120]{1,0:T(8,128)(2,1)} %reshape.224, bf16[2,5120,512]{2,1,0:T(8,128)(2,1)} %all-gather.2.cloned.1.call-done), kind=kOutput, calls=%fused_computation.20 | convolution fusion | flops 671088640 | bytes 6815744 | tf_op jit(solution)/shard_map/dot_general | solution.py:48
  246.4 0.8 copy.52
  247.3 1.0 reshape.225
  248.3 0.9 multiply_reduce_fusion
  249.2 0.9 copy.53
  250.1 0.6 add_sqrt_fusion
  250.8 1.4 copy.54
  252.2 1.0 copy_divide_fusion
  253.3 1.2 subtract_convert_fusion
  254.4 5.5 %fusion.46 = (f32[32,4,8,4]{2,3,1,0:T(4,128)S(1)}, f32[32,4,8,4,4]{2,4,3,1,0:T(4,128)S(1)}) fusion(bf16[32,4,4,64]{3,1,2,0:T(4,128)(2,1)S(1)} %get-tuple-element.30, bf16[32,4,4,64]{3,1,2,0:T(4,128)(2,1)S(1)} %get-tuple-element.29, pred[4,4]{1,0:T(4,128)(4,1)} %iota_compare_fusion.3, bf16[32,4,32,128]{3,2,1,0:T(8,128)(2,1)S(1)} %copy-done), kind=kOutput, calls=%fused_computation.75 | convolution fusion | flops 4501504 | bytes 1261584 | tf_op jit(solution)/shard_map/rsgqh,rtgh->rgqst/dot_general | solution.py:92
  260.0 2.3 fusion.10
  262.3 1.7 fusion.26
  264.0 0.7 convert_element_type.71
  264.7 1.1 add.71
  265.8 2.2 fusion.27
  268.4 2.0 fusion.6
  271.1 0.8 convolution_convert_fusion
  271.8 2.9 copy.65
  274.8 6.1 %all-to-all-start = ((bf16[32,2,4,4096]{3,2,1,0:T(4,128)(2,1)}), bf16[32,2,4,4096]{3,2,1,0:T(4,128)(2,1)S(1)}, u32[]{:S(2)}, u32[]{:S(2)}) async-start(bf16[32,2,4,4096]{3,2,1,0:T(4,128)(2,1)} %copy.65), calls=%async_computation | async-start | bytes 4194304 | tf_op jit(solution)/shard_map/all_to_all | solution.py:125
  280.9 0.7 convert_element_type.68
  281.6 1.0 copy.57
  282.8 0.8 copy.66
  283.6 45.9 %all-to-all-done = bf16[32,2,4,4096]{3,2,1,0:T(4,128)(2,1)S(1)} async-done(((bf16[32,2,4,4096]{3,2,1,0:T(4,128)(2,1)}), bf16[32,2,4,4096]{3,2,1,0:T(4,128)(2,1)S(1)}, u32[]{:S(2)}, u32[]{:S(2)}) %all-to-all-start) | async-done | bytes 2097184 | tf_op jit(solution)/shard_map/all_to_all | solution.py:125
  329.5 1.3 copy.98
  (41 shorter events, 2.4 us)
Async XLA Ops:
  7.2 6.6 %copy-start = (bf16[32,4,32,128]{3,2,1,0:T(8,128)(2,1)S(1)}, bf16[32,4,32,128]{3,2,1,0:T(8,128)(2,1)}, u32[]{:S(2)}) copy-start(bf16[32,4,32,128]{3,2,1,0:T(8,128)(2,1)} %param.16) | copy-start | bytes 3145732
  7.2 2.3 copy-start.1
  7.2 4.0 %copy-start.11 = (s32[32]{0:T(128)S(1)}, s32[32]{0:T(128)}, u32[]{:S(2)}) copy-start(s32[32]{0:T(128)} %param.21) | copy-start | bytes 388
  7.2 4.2 %copy-start.13 = (s32[32]{0:T(128)S(1)}, s32[32]{0:T(128)}, u32[]{:S(2)}) copy-start(s32[32]{0:T(128)} %param.20) | copy-start | bytes 388
  7.2 5.2 %copy-start.9 = (s32[32]{0:T(128)S(1)}, s32[32]{0:T(128)}, u32[]{:S(2)}) copy-start(s32[32]{0:T(128)} %param.19) | copy-start | bytes 388
  7.2 230.2 %all-gather.2.cloned.1.call-start = ((), (), s32[]{:S(2)}) async-start(), calls=%async_computation.1 | async-start | bytes 10567680 | tf_op jit(solution)/shard_map/all_gather | solution.py:77
  253.2 6.7 %copy-start.7 = (f32[32,4,8,4]{2,3,1,0:T(4,128)S(1)}, f32[32,4,8,4]{2,3,1,0:T(4,128)}, u32[]{:S(2)}) copy-start(f32[32,4,8,4]{2,3,1,0:T(4,128)} %get-tuple-element.33) | copy-start | bytes 49156
  254.4 5.6 %copy-start.3 = (bf16[32,4,4,64]{3,1,2,0:T(4,128)(2,1)}, bf16[32,4,4,64]{3,1,2,0:T(4,128)(2,1)S(1)}, u32[]{:S(2)}) copy-start(bf16[32,4,4,64]{3,1,2,0:T(4,128)(2,1)S(1)} %get-tuple-element.29) | copy-start | bytes 196612
  254.4 5.6 %copy-start.5 = (bf16[32,4,4,64]{3,1,2,0:T(4,128)(2,1)}, bf16[32,4,4,64]{3,1,2,0:T(4,128)(2,1)S(1)}, u32[]{:S(2)}) copy-start(bf16[32,4,4,64]{3,1,2,0:T(4,128)(2,1)S(1)} %get-tuple-element.30) | copy-start | bytes 196612
  259.9 2.4 copy-start.2
  265.8 2.6 copy-start.12
  270.3 0.7 copy-start.8
  270.3 0.7 copy-start.10
  274.8 7.8 %copy-start.4 = (bf16[32,4,4,64]{3,1,2,0:T(4,128)(2,1)S(1)}, bf16[32,4,4,64]{3,1,2,0:T(4,128)(2,1)}, u32[]{:S(2)}) copy-start(bf16[32,4,4,64]{3,1,2,0:T(4,128)(2,1)} %copy-done.3) | copy-start | bytes 196612
  274.8 7.8 %copy-start.6 = (bf16[32,4,4,64]{3,1,2,0:T(4,128)(2,1)S(1)}, bf16[32,4,4,64]{3,1,2,0:T(4,128)(2,1)}, u32[]{:S(2)}) copy-start(bf16[32,4,4,64]{3,1,2,0:T(4,128)(2,1)} %copy-done.5) | copy-start | bytes 196612
  274.8 54.8 %all-to-all-start = ((bf16[32,2,4,4096]{3,2,1,0:T(4,128)(2,1)}), bf16[32,2,4,4096]{3,2,1,0:T(4,128)(2,1)S(1)}, u32[]{:S(2)}, u32[]{:S(2)}) async-start(bf16[32,2,4,4096]{3,2,1,0:T(4,128)(2,1)} %copy.65), calls=%async_computation | async-start | bytes 4194304 | tf_op jit(solution)/shard_map/all_to_all | solution.py:125
Sparse Core Ops, SparseCore 0:
  10.4 226.9 all-gather.1
where the time goes:
time: 340 us; the launch traced here: 338 us
  waiting for transfers between devices  264 us (78%)
  matrix products  24.6 us (7%)
  other arithmetic  14.3 us (4%)
  between operations  14.3 us (4%)
  local copies, waits for them, and re-layouts  14 us (4%)
  starting transfers between devices  6.14 us (2%)
    all_gather x1, waiting for transfers between devices, on_device(): lax.all_gather(weight_bf, ('fsdp', 'gen'), axis=1, tiled=True)  218 us
    all_to_all x1, waiting for transfers between devices, on_device(): lax.all_to_all(outgoing, 'fsdp', split_axis=0, concat_axis=0, tiled=True)  45.9 us
  transfers between devices with their start and end apart: 2, of which 2 were waited for; matrix products, arithmetic and copies ran while one was open for 4% of the time, Pallas kernels for 0%

commit v1 on v0

v1 whole, which is shorter than its diff:
```python
import functools
import jax
import jax.numpy as jnp
from jax import lax
from jax.experimental import pallas as pl
from jax.experimental.pallas import tpu as pltpu
from jax.sharding import Mesh, PartitionSpec as P

beta_one = 0.9
beta_two = 0.95
adam_eps = 1e-08
learn_rate = 0.002
weight_decay = 0.1
adam_step = 10.0
rope_theta = 1000000.0
norm_eps = 1e-06
masked_score = -1e30

N_Y = 4
N_Z = 8
N_GEN = 4
N_FSDP = N_Y * N_Z
HEAD = 128
HEADS = 4
STEPS = 4
ROLL = 32
TOKENS = ROLL * STEPS
CACHE = 128
ROWS = 40
DEPTH = 1280
SLOTS = 2
SCALE = HEAD ** (-0.5)
F32 = jnp.float32
BF16 = jnp.bfloat16
VMEM_BYTES = 48 * 1024 * 1024


def params(**more):
    return pltpu.CompilerParams(vmem_limit_bytes=VMEM_BYTES, **more)


def whole():
    return pl.BlockSpec(memory_space=pltpu.VMEM)


def iota(shape, axis):
    return lax.broadcasted_iota(jnp.int32, shape, axis)


def adam_kernel(master_ref, grad_ref, first_ref, second_ref, m_out, f_out, s_out, w_out):
    for kv in range(2):
        grad = grad_ref[kv]
        master = master_ref[kv]
        first = beta_one * first_ref[kv] + (1.0 - beta_one) * grad
        second = beta_two * second_ref[kv] + (1.0 - beta_two) * grad * grad
        first_hat = first / (1.0 - beta_one**adam_step)
        second_hat = second / (1.0 - beta_two**adam_step)
        master = master - learn_rate * (
            first_hat / (jnp.sqrt(second_hat) + adam_eps) + weight_decay * master
        )
        f_out[kv] = first
        s_out[kv] = second
        m_out[kv] = master
        rounded = master.astype(BF16)
        for q in range(N_GEN):
            piece = rounded[:, q * HEAD : (q + 1) * HEAD]
            for z in range(N_Z):
                w_out[z, q, :, kv * HEAD : (kv + 1) * HEAD] = piece


def adam(master, grad, first, second):
    shape = jax.ShapeDtypeStruct(master.shape, F32)
    return pl.pallas_call(
        adam_kernel,
        out_shape=(shape, shape, shape, jax.ShapeDtypeStruct((N_Z, N_GEN, ROWS, 2 * HEAD), BF16)),
        in_specs=[whole()] * 4,
        out_specs=(whole(),) * 4,
        compiler_params=params(),
        name="adam",
    )(master, grad, first, second)


OLD_BLOCK = 4


def old_kernel(prefix, dest, slot, q_ref, k_ref, v_ref, out_ref, lse_ref, qp_ref, ok_ref):
    step = pl.program_id(0)
    span = CACHE * HEADS

    @pl.when(step == 0)
    def _():
        out_ref[...] = jnp.zeros_like(out_ref)
        row, col = iota((TOKENS, span), 0), iota((TOKENS, span), 1)
        ok_ref[...] = jnp.where(col % HEADS == row // 32, col, CACHE * HEADS)

    row, col = iota((TOKENS, TOKENS), 0), iota((TOKENS, TOKENS), 1)
    perm = ((col % 32 == row // 4) & (col // 32 == row % 4)).astype(BF16)
    eye = row == col
    place = ok_ref[...]
    lses = []
    for n in range(OLD_BLOCK):
        r = step * OLD_BLOCK + n
        query = jnp.dot(perm, q_ref[n], preferred_element_type=F32).astype(BF16)
        qp_ref[n] = query
        score = lax.dot_general(
            query, k_ref[n], (((1,), (1,)), ((), ())), preferred_element_type=F32
        )
        score = jnp.where(place < prefix[r] * HEADS, score * SCALE, masked_score)
        top = jnp.max(score, axis=1, keepdims=True)
        weight = jnp.exp(score - top)
        total = jnp.sum(weight, axis=1, keepdims=True)
        mixed = jnp.dot(weight.astype(BF16), v_ref[n], preferred_element_type=F32)
        out_ref[dest[r], slot[r]] = (mixed / total).astype(BF16)
        lse = top + jnp.log(total)
        lses.append(jnp.sum(jnp.where(eye, lse, 0.0), axis=0, keepdims=True))
    for n in range(0, OLD_BLOCK, 2):
        lse_ref[pl.ds((step * OLD_BLOCK + n) // 2, 1), :] = jnp.concatenate(
            [lses[n], lses[n + 1]], axis=1
        )


def old_attention(prefix, dest, slot, queries, keys, values):
    span = CACHE * HEADS
    return pl.pallas_call(
        old_kernel,
        grid_spec=pltpu.PrefetchScalarGridSpec(
            num_scalar_prefetch=3,
            grid=(ROLL // OLD_BLOCK,),
            in_specs=[
                pl.BlockSpec((OLD_BLOCK, TOKENS, HEAD), lambda i, *_: (i, 0, 0)),
                pl.BlockSpec((OLD_BLOCK, span, HEAD), lambda i, *_: (i, 0, 0)),
                pl.BlockSpec((OLD_BLOCK, span, HEAD), lambda i, *_: (i, 0, 0)),
            ],
            out_specs=(
                pl.BlockSpec((N_FSDP, SLOTS, TOKENS, HEAD), lambda i, *_: (0, 0, 0, 0)),
                pl.BlockSpec((ROLL // 2, 2 * TOKENS), lambda i, *_: (0, 0)),
                pl.BlockSpec((OLD_BLOCK, TOKENS, HEAD), lambda i, *_: (i, 0, 0)),
            ),
            scratch_shapes=[pltpu.VMEM((TOKENS, span), jnp.int32)],
        ),
        out_shape=(
            jax.ShapeDtypeStruct((N_FSDP, SLOTS, TOKENS, HEAD), BF16),
            jax.ShapeDtypeStruct((ROLL // 2, 2 * TOKENS), F32),
            jax.ShapeDtypeStruct((ROLL, TOKENS, HEAD), BF16),
        ),
        compiler_params=params(),
        cost_estimate=pl.CostEstimate(
            flops=2 * 2 * ROLL * TOKENS * span * HEAD,
            bytes_accessed=13 * 1024 * 1024,
            transcendentals=ROLL * TOKENS * span,
        ),
        name="old_attention",
    )(prefix, dest, slot, queries, keys, values)


def project_kernel(me, w_ref, x0, x1, x2, x3, out_ref):
    weight = w_ref[...]
    for j, x in enumerate((x0, x1, x2, x3)):
        out_ref[0, me[0] ^ j] = jnp.dot(
            x[0], weight, preferred_element_type=F32
        ).astype(BF16)


def project(me, weight, pieces):
    return pl.pallas_call(
        project_kernel,
        grid_spec=pltpu.PrefetchScalarGridSpec(
            num_scalar_prefetch=1,
            grid=(N_Y,),
            in_specs=[pl.BlockSpec((DEPTH, 2 * HEAD), lambda i, *_: (0, 0))]
            + [pl.BlockSpec((1, TOKENS, DEPTH), lambda i, *_: (i, 0, 0))] * 4,
            out_specs=pl.BlockSpec((1, N_GEN, TOKENS, 2 * HEAD), lambda i, *_: (i, 0, 0, 0)),
        ),
        out_shape=jax.ShapeDtypeStruct((N_Y, N_GEN, TOKENS, 2 * HEAD), BF16),
        compiler_params=params(),
        cost_estimate=pl.CostEstimate(
            flops=2 * N_Y * N_GEN * TOKENS * DEPTH * 2 * HEAD,
            bytes_accessed=7 * 1024 * 1024,
            transcendentals=0,
        ),
        name="project",
    )(me, weight, *pieces)


def fresh_kernel(
    dest, slot, lengths, part_ref, cos_ref, sin_ref, qp_ref, lse_ref, kv_ref, late_ref, kf, vf, wf
):
    cosine, sine = cos_ref[...], sin_ref[...]
    for g in range(HEADS):
        total = part_ref[0, g].astype(F32)
        for y in range(1, N_Y):
            total = total + part_ref[y, g].astype(F32)
        key, value = total[:, :HEAD], total[:, HEAD:]
        key = key / jnp.sqrt(jnp.mean(key * key, axis=-1, keepdims=True) + norm_eps)
        key = key * cosine + pltpu.roll(key, HEAD // 2, 1) * sine
        key, value = key.astype(BF16), value.astype(BF16)
        kv_ref[0, g] = key
        kv_ref[1, g] = value
        kf[g] = key.astype(F32)
        vf[g] = value.astype(F32)
    late_ref[...] = jnp.zeros_like(late_ref)
    wf[...] = jnp.zeros_like(wf)

    row, col = iota((32, 256), 0), iota((32, 256), 1)
    own = (
        (row // 8 == (col % 128) // 32)
        & ((row % 8) // 4 == col // 128)
        & (row % 4 <= col % 4)
    )
    lane = iota((1, 256), 1)
    row8 = iota((8, 128), 0)

    def pair(p, carry):
        keys = jnp.concatenate(
            [kf[g, pl.ds(pl.multiple_of(p * 8, 8), 8), :] for g in range(HEADS)], axis=0
        ).astype(BF16)
        query = qp_ref[pl.ds(2 * p, 2)].reshape(2 * TOKENS, HEAD)
        score = lax.dot_general(
            keys, query, (((1,), (1,)), ((), ())), preferred_element_type=F32
        )
        score = jnp.where(own, score * SCALE, masked_score)
        old = lse_ref[pl.ds(p, 1), :]
        top = jnp.maximum(jnp.max(score, axis=0, keepdims=True), old)
        weight = jnp.exp(score - top)
        alpha = jnp.exp(old - top)
        total = jnp.sum(weight, axis=0, keepdims=True) + alpha
        kept = (lane % STEPS) < jnp.where(lane < 128, lengths[2 * p], lengths[2 * p + 1])
        scale = jnp.where(kept, 1.0 / total, 0.0)
        weight = weight * scale
        alpha = alpha * scale
        weight = weight[0:8] + weight[8:16] + weight[16:24] + weight[24:32]
        vals = [vf[g, pl.ds(pl.multiple_of(p * 8, 8), 8), :] for g in range(HEADS)]
        for rr in range(2):
            r = 2 * p + rr
            d, j = dest[r], slot[r]
            mine = weight[:, rr * 128 : (rr + 1) * 128]
            if rr:
                mine = pltpu.roll(mine, 4, 0)
            mine = jnp.where(row8 == 4, alpha[:, rr * 128 : (rr + 1) * 128], mine)
            wf[d, pl.ds(pl.multiple_of(j * 8, 8), 8), :] = mine
            tiles = []
            for g in range(0, HEADS, 2):
                first, second = vals[g], vals[g + 1]
                if rr:
                    first = pltpu.roll(first, 4, 0)
                else:
                    second = pltpu.roll(second, 4, 0)
                tiles.append(jnp.where(row8 < 4, first, second))
            late_ref[d, pl.ds(pl.multiple_of(j * 16, 16), 16), :] = jnp.concatenate(
                tiles, axis=0
            ).astype(BF16)
        return carry

    lax.fori_loop(0, ROLL // 2, pair, 0, unroll=4)
    late_ref[:, 32:48, :] = wf[...].astype(BF16)


def fresh(dest, slot, lengths, parts, cosine, sine, queries, lse):
    smem = pl.BlockSpec(memory_space=pltpu.SMEM)
    return pl.pallas_call(
        fresh_kernel,
        in_specs=[smem] * 3 + [whole()] * 5,
        out_specs=(whole(), whole()),
        out_shape=(
            jax.ShapeDtypeStruct((2, HEADS, TOKENS, HEAD), BF16),
            jax.ShapeDtypeStruct((N_FSDP, 48, HEAD), BF16),
        ),
        scratch_shapes=[
            pltpu.VMEM((HEADS, TOKENS, HEAD), F32),
            pltpu.VMEM((HEADS, TOKENS, HEAD), F32),
            pltpu.VMEM((N_FSDP, 16, HEAD), F32),
        ],
        compiler_params=params(),
        cost_estimate=pl.CostEstimate(
            flops=2 * 32 * 32 * 256 * 128, bytes_accessed=3 * 1024 * 1024, transcendentals=1000000
        ),
        name="fresh",
    )(dest, slot, lengths, parts, cosine, sine, queries, lse)


JOIN_BLOCK = 8


def join_kernel(old_ref, late_ref, out_ref):
    row, col = iota((TOKENS, TOKENS), 0), iota((TOKENS, TOKENS), 1)
    eye = row == col
    row8 = iota((8, 128), 0)
    row16, lane = iota((16, 128), 0), iota((16, 128), 1)
    same = lane // 32 == row16 // 4
    for n in range(JOIN_BLOCK):
        tile = late_ref[n, 32:48, :].astype(F32)
        for j in range(SLOTS):
            mine = tile[j * 8 : (j + 1) * 8]
            alpha = mine[4:5]
            diag = jnp.where(eye, alpha, 0.0).astype(BF16)
            mixed = jnp.dot(diag, old_ref[n, j], preferred_element_type=F32)
            both = jnp.where(row8 < 4, mine, pltpu.roll(mine, 4, 0))
            weight = jnp.where(same, jnp.concatenate([both, both], axis=0), 0.0).astype(BF16)
            value = late_ref[n, j * 16 : (j + 1) * 16, :]
            mixed = mixed + lax.dot_general(
                weight, value, (((0,), (0,)), ((), ())), preferred_element_type=F32
            )
            out_ref[n, j] = mixed.astype(BF16)


def join(old, late):
    return pl.pallas_call(
        join_kernel,
        grid=(N_FSDP // JOIN_BLOCK,),
        in_specs=[
            pl.BlockSpec((JOIN_BLOCK, SLOTS, TOKENS, HEAD), lambda i: (i, 0, 0, 0)),
            pl.BlockSpec((JOIN_BLOCK, 48, HEAD), lambda i: (i, 0, 0)),
        ],
        out_specs=pl.BlockSpec((JOIN_BLOCK, SLOTS, TOKENS, HEAD), lambda i: (i, 0, 0, 0)),
        out_shape=jax.ShapeDtypeStruct((N_FSDP, SLOTS, TOKENS, HEAD), BF16),
        compiler_params=params(),
        cost_estimate=pl.CostEstimate(
            flops=2 * 64 * 144 * 128 * 128, bytes_accessed=5 * 1024 * 1024, transcendentals=0
        ),
        name="join",
    )(old, late)


def turn_tables(prefix_lengths):
    half_size = HEAD // 2
    exponent = -2.0 * jnp.arange(half_size).astype(F32) / HEAD
    inverse_freq = jnp.power(jnp.float32(rope_theta), exponent)
    positions = prefix_lengths[:, None] + jnp.arange(STEPS, dtype=jnp.int32)[None, :]
    angle = positions.reshape(TOKENS, 1).astype(F32) * inverse_freq
    cosine, sine = jnp.cos(angle), jnp.sin(angle)
    return (
        jnp.concatenate([cosine, cosine], axis=-1),
        jnp.concatenate([-sine, sine], axis=-1),
    )


def at(x):
    return (x % 2) * 2 + x // 2


def on_device(
    master_weight,
    gradient,
    first_moment,
    second_moment,
    new_inputs,
    queries,
    cache_keys,
    cache_values,
    prefix_lengths,
    rollout_lengths,
    destinations,
):
    new_master, new_first, new_second, blocks = adam(
        master_weight, gradient, first_moment, second_moment
    )
    weight = lax.all_to_all(
        blocks.reshape(N_Z * N_GEN, ROWS, 2 * HEAD), ("z", "xl", "c"), 0, 0, tiled=True
    ).reshape(DEPTH, 2 * HEAD)

    columns = new_inputs.reshape(TOKENS, N_Y, DEPTH).transpose(1, 0, 2)
    own = lax.all_to_all(columns, "y", 0, 0, tiled=True)
    ring = [(at(x), at((x + 1) % 4)) for x in range(4)]
    back = [(at(x), at((x + 3) % 4)) for x in range(4)]
    swap = [(0, 1), (1, 0)]
    far = jnp.concatenate(
        [
            lax.ppermute(own[: N_Y // 2], ("xl", "tp"), ring),
            lax.ppermute(own[N_Y // 2 :], ("xl", "tp"), back),
        ],
        axis=0,
    )
    near = lax.ppermute(own, "c", swap)
    both = lax.ppermute(far, "c", swap)

    same_dest = destinations[:, None] == destinations[None, :]
    earlier = jnp.arange(ROLL)[None, :] < jnp.arange(ROLL)[:, None]
    slot_rank = jnp.sum((same_dest & earlier).astype(jnp.int32), axis=1)
    old_rows, lse, ordered = old_attention(
        prefix_lengths,
        destinations,
        slot_rank,
        queries.reshape(ROLL, TOKENS, HEAD),
        cache_keys.reshape(ROLL, CACHE * HEADS, HEAD),
        cache_values.reshape(ROLL, CACHE * HEADS, HEAD),
    )
    old_in = lax.all_to_all(old_rows, ("y", "z"), 0, 0, tiled=True)

    me = (lax.axis_index("xl") * 2 + lax.axis_index("c")).reshape(1)
    parts = project(me, weight, (own, near, far, both))
    parts = lax.all_to_all(
        parts.reshape(N_Y * N_GEN, TOKENS, 2 * HEAD), ("y", "xl", "c"), 0, 0, tiled=True
    ).reshape(N_Y, N_GEN, TOKENS, 2 * HEAD)
    cosine, sine = turn_tables(prefix_lengths)
    fresh_parts, late = fresh(
        destinations, slot_rank, rollout_lengths, parts, cosine, sine, ordered, lse
    )
    late_in = lax.all_to_all(late, ("y", "z"), 0, 0, tiled=True)
    fresh_kv = fresh_parts.reshape(2, HEADS, ROLL, STEPS, HEAD).transpose(2, 3, 0, 1, 4)
    joined = join(old_in, late_in)
    returned = joined.reshape(N_FSDP, SLOTS, 8 * HEADS, STEPS, HEAD).transpose(0, 1, 3, 2, 4)
    returned_rows = returned.reshape(1, 1, N_FSDP, SLOTS, STEPS, 8 * HEADS * HEAD)
    return (new_master, new_first, new_second, fresh_kv, returned_rows)


def solution(mesh):
    fine = Mesh(mesh.devices.reshape(N_Y, N_Z, 2, 2, 2), ("y", "z", "xl", "c", "tp"))
    group = ("y", "z", "xl", "c")
    rows = P(None, group, "tp")
    in_specs = (
        rows,
        rows,
        rows,
        rows,
        P(group, None, None),
        P(group, None, "tp", None),
        P(group, None, "tp", None),
        P(group, None, "tp", None),
        P(group),
        P(group),
        P(group),
    )
    out_specs = (
        rows,
        rows,
        rows,
        P(group, None, None, "tp", None),
        P(("y", "z"), ("xl", "c"), None, None, None, "tp"),
    )
    return jax.shard_map(
        on_device, mesh=fine, in_specs=in_specs, out_specs=out_specs, check_vma=False
    )
```

time: 340 us -> 183 us (0.54)
  waiting for transfers between devices: 264 us -> 84.4 us
  starting transfers between devices: 6.14 us -> 35.5 us
  Pallas kernels: 0 us -> 26.1 us
  matrix products: 24.6 us -> 0 us
  blocking collectives: 0 us -> 21.8 us
  other arithmetic: 14.3 us -> 0.67 us
  between operations: 14.3 us -> 0.81 us
  local copies, waits for them, and re-layouts: 14 us -> 9.64 us
    all_gather x1 -> x0, waiting for transfers between devices: 218 us -> none  [on_device(): lax.all_gather(weight_bf, ('fsdp', 'gen'), axis=1, tiled=True)]
    all_to_all x1 -> x4, waiting for transfers between devices: 45.9 us -> 74.1 us  [the longest x1 44 us: on_device(): old_in = lax.all_to_all(old_rows, ('y', 'z'), 0, 0, tiled=True)]
    pallas_call x0 -> x5, Pallas kernels: none -> 26.1 us  [the longest x1 15.6 us: old_attention(): pl.pallas_call(old_kernel, grid_spec=pltpu.PrefetchScalarGridSpec(num_sca...]
    dot_general x7 -> x0, matrix products: 24.6 us -> none  [the longest x1 5.46 us: on_device(): jnp.einsum('rsgqh,rtgh->rgqst', grouped, fresh_keys, preferred_element_ty...]
    all_to_all x0 -> x1, blocking collectives: none -> 21.8 us  [on_device(): own = lax.all_to_all(columns, 'y', 0, 0, tiled=True)]
    all_to_all x1 -> x4, starting transfers between devices: 6.1 us -> 27.4 us  [the longest x1 9.66 us: on_device(): lax.all_to_all(blocks.reshape(N_Z * N_GEN, ROWS, 2 * HEAD), ('z', 'xl', '...]
    ppermute x0 -> x4, waiting for transfers between devices: none -> 10.4 us  [the longest x1 10.4 us: on_device(): lax.ppermute(own[:N_Y // 2], ('xl', 'tp'), ring)]
    ppermute x0 -> x4, starting transfers between devices: none -> 8.16 us  [the longest x1 2.9 us: on_device(): both = lax.ppermute(far, 'c', swap)]
  transfers between devices with their start and end apart: 2 -> 8, of which waited for: 2 -> 4; matrix products, arithmetic and copies ran while one was open for 4% -> 1% of each run, Pallas kernels for 0% -> 11%
where the time goes in v1:
time: 183 us; the launch traced here: 179 us
  waiting for transfers between devices  84.4 us (46%)
  starting transfers between devices  35.5 us (19%)
  Pallas kernels  26.1 us (14%)
  blocking collectives  21.8 us (12%)
  local copies, waits for them, and re-layouts  9.64 us (5%)
    all_to_all x1, waiting for transfers between devices, on_device(): old_in = lax.all_to_all(old_rows, ('y', 'z'), 0, 0, tiled=True)  44 us
    all_to_all x1, blocking collectives, on_device(): own = lax.all_to_all(columns, 'y', 0, 0, tiled=True)  21.8 us
    all_to_all x1, waiting for transfers between devices, on_device(): lax.all_to_all(blocks.reshape(N_Z * N_GEN, ROWS, 2 * HEAD), ('z', 'xl', '...  19.6 us
    pallas_call x1, Pallas kernels, old_attention(): pl.pallas_call(old_kernel, grid_spec=pltpu.PrefetchScalarGridSpec(num_sca...  15.6 us
    all_to_all x1, waiting for transfers between devices, on_device(): late_in = lax.all_to_all(late, ('y', 'z'), 0, 0, tiled=True)  10.5 us
    ppermute x1, waiting for transfers between devices, on_device(): lax.ppermute(own[:N_Y // 2], ('xl', 'tp'), ring)  10.4 us
    all_to_all x1, starting transfers between devices, on_device(): lax.all_to_all(blocks.reshape(N_Z * N_GEN, ROWS, 2 * HEAD), ('z', 'xl', '...  9.66 us
    all_to_all x1, starting transfers between devices, on_device(): late_in = lax.all_to_all(late, ('y', 'z'), 0, 0, tiled=True)  7.62 us
  transfers between devices with their start and end apart: 8, of which 4 were waited for; matrix products, arithmetic and copies ran while one was open for 1% of the time, Pallas kernels for 11%

profile of v1, /device:TPU:1, one launch (start us, length us, event | category | flops | bytes accessed | tf_op | source)
XLA Modules:
  0.0 179.0 jit_solution(11973665855632128355)
XLA Ops:
  0.6 3.0 %reshape.75 = bf16[128,4,1280]{2,1,0:T(4,128)(2,1)S(1)} reshape(bf16[32,4,5120]{2,1,0:T(4,128)(2,1)} %param.15) | data formatting | bytes 2621440 | tf_op jit(solution)/shard_map/reshape | solution.py:361
  3.6 0.1 copy.26
  3.7 21.8 %all_to_all.25.x0 = bf16[4,128,1280]{2,1,0:T(8,128)(2,1)S(1)} all-to-all(bf16[4,128,1280]{2,1,0:T(8,128)(2,1)S(1)} %bitcast.26), channel_id=1, replica_groups=mesh['y'=4,'z'=8,'xl'=2,'c'=2,'tp'=2] {'y'}, dimensions={0} | all-to-all | bytes 2621440 | tf_op jit(solution)/shard_map/all_to_all | solution.py:362
  25.5 0.1 fusion.2
  25.6 1.3 collective-permute-start.1
  26.9 1.5 collective-permute-start.2
  28.5 2.4 %collective-permute-start = (bf16[4,128,1280]{2,1,0:T(8,128)(2,1)S(1)}, bf16[4,128,1280]{2,1,0:T(8,128)(2,1)}, u32[]{:S(2)}, u32[]{:S(2)}) collective-permute-start(bf16[4,128,1280]{2,1,0:T(8,128)(2,1)S(1)} %all_to_all.25.x0), channel_id=1, source_target_pairs={{0,2},{2,0},{1,3},{3,1},{4,6},{6,4},{5,7},{7,5},{8,10},{10,8},{9,1... | collective-permute-start | bytes 3932168 | tf_op jit(solution)/shard_map/ppermute | solution.py:373
  30.9 10.4 %collective-permute-done.1 = bf16[2,128,1280]{2,1,0:T(8,128)(2,1)S(1)} collective-permute-done((bf16[2,128,1280]{2,1,0:T(8,128)(2,1)S(1)}, bf16[2,128,1280]{2,1,0:T(8,128)(2,1)S(1)}, u32[]{:S(2)}, u32[]{:S(2)}) %collective-permute-start.1) | collective-permute-done | bytes 655392 | tf_op jit(solution)/shard_map/ppermute | solution.py:368
  41.4 2.9 %collective-permute-start.3 = (bf16[4,128,1280]{2,1,0:T(8,128)(2,1)S(1)}, bf16[4,128,1280]{2,1,0:T(8,128)(2,1)}, u32[]{:S(2)}, u32[]{:S(2)}) collective-permute-start(bf16[4,128,1280]{2,1,0:T(8,128)(2,1)S(1)} %constant_dynamic-update-slice_fusion.x2), channel_id=1, source_target_pairs={{0,2},{2,0},{1,3},{3,1},{4,6},{6,4},{5,7},{7,5},{8,10},{10,8},{9,1... | collective-permute-start | bytes 3932168 | tf_op jit(solution)/shard_map/ppermute | solution.py:374
  44.3 0.9 adam.1
  45.2 0.8 copy-done.5
  46.0 9.7 %all-to-all-start = ((bf16[32,40,256]{2,1,0:T(8,128)(2,1)}), bf16[32,40,256]{2,1,0:T(8,128)(2,1)S(1)}, u32[]{:S(2)}, u32[]{:S(2)}) async-start(bf16[32,40,256]{2,1,0:T(8,128)(2,1)} %bitcast.24), calls=%async_computation | async-start | bytes 1310720 | tf_op jit(solution)/shard_map/all_to_all | solution.py:357
  55.7 19.6 %all-to-all-done = bf16[32,40,256]{2,1,0:T(8,128)(2,1)S(1)} async-done(((bf16[32,40,256]{2,1,0:T(8,128)(2,1)}), bf16[32,40,256]{2,1,0:T(8,128)(2,1)S(1)}, u32[]{:S(2)}, u32[]{:S(2)}) %all-to-all-start) | async-done | bytes 655392 | tf_op jit(solution)/shard_map/all_to_all | solution.py:357
  75.3 3.8 %project.1 = bf16[4,4,128,256]{3,2,1,0:T(8,128)(2,1)S(1)} custom-call(s32[1]{0:T(128)} %bitcast.me, bf16[1280,256]{1,0:T(8,128)(2,1)S(1)} %bitcast.22, bf16[4,128,1280]{2,1,0:T(8,128)(2,1)S(1)} %all_to_all.25.x0, bf16[4,128,1280]{2,1,0:T(8,128)(2,1)} %collective-permute-done.x1, bf16[4,128,1280]{2,1,0:T(8,128)(2,1)S(1)} %constant_dynamic-update-slice_fusion.x2, ...), custom_call_target="tpu_custom_call" | custom-call | flops 1342177280 | bytes 7340032 | tf_op jit(solution)/shard_map/project/pallas_call | solution.py:165
  79.1 1.0 copy-done
  80.2 4.9 %all-to-all-start.2 = ((bf16[16,128,256]{2,1,0:T(8,128)(2,1)}), bf16[16,128,256]{2,1,0:T(8,128)(2,1)S(1)}, u32[]{:S(2)}, u32[]{:S(2)}) async-start(bf16[16,128,256]{2,1,0:T(8,128)(2,1)} %bitcast.21), calls=%async_computation.2 | async-start | bytes 2097152 | tf_op jit(solution)/shard_map/all_to_all | solution.py:391
  85.1 0.2 convert_reduce_fusion.slot
  85.3 15.6 %old_attention.1 = (bf16[32,2,128,128]{3,2,1,0:T(8,128)(2,1)S(1)}, f32[16,256]{1,0:T(8,128)S(1)}, bf16[32,128,128]{2,1,0:T(8,128)(2,1)S(1)}) custom-call(s32[32]{0:T(128)S(1)} %copy-done.11, s32[32]{0:T(128)S(1)} %copy-done.10, s32[32]{0:T(128)S(1)} %convert_reduce_fusion.slot, bf16[32,128,128]{2,1,0:T(8,128)(2,1)S(1)} %bitcast.23, ...), custom_call_target="tpu_custom_call" | custom-call | flops 1073741824 | bytes 13631488 | tf_op jit(solution)/shard_map/old_attention/pallas_call | solution.py:124
  100.9 1.3 copy-done.1
  102.2 1.0 copy-done.3
  103.2 5.2 %all-to-all-start.3 = ((bf16[32,2,128,128]{3,2,1,0:T(8,128)(2,1)}), bf16[32,2,128,128]{3,2,1,0:T(8,128)(2,1)S(1)}, u32[]{:S(2)}, u32[]{:S(2)}) async-start(bf16[32,2,128,128]{3,2,1,0:T(8,128)(2,1)} %copy-done.1), calls=%async_computation.3 | async-start | bytes 4194304 | tf_op jit(solution)/shard_map/all_to_all | solution.py:387
  108.3 0.1 add_convert_fusion
  108.4 0.1 convert_element_type.23
  108.5 0.3 fusion
  108.9 0.1 pad_maximum_fusion
  109.0 1.2 copy-done.4
  110.2 2.7 %fresh.1 = (bf16[2,4,128,128]{3,2,1,0:T(8,128)(2,1)S(1)}, bf16[32,48,128]{2,1,0:T(8,128)(2,1)}) custom-call(s32[32]{0:T(128)S(1)} %copy-done.10, s32[32]{0:T(128)S(1)} %convert_reduce_fusion.slot, s32[32]{0:T(128)S(1)} %copy-done.12, bf16[4,4,128,256]{3,2,1,0:T(8,128)(2,1)S(1)} %bitcast.20, f32[128,128]{1,0:T(8,128)S(1)} %get-tuple-element.28.cos_ref, ...), custom_call_target="tpu_custom_call" | custom-call | flops 67108864 | bytes 3145728 | tf_op jit(solution)/shard_map/fresh/pallas_call | solution.py:260
  112.9 44.0 %all-to-all-done.3.old_ref = bf16[32,2,128,128]{3,2,1,0:T(8,128)(2,1)S(1)} async-done(((bf16[32,2,128,128]{3,2,1,0:T(8,128)(2,1)}), bf16[32,2,128,128]{3,2,1,0:T(8,128)(2,1)S(1)}, u32[]{:S(2)}, u32[]{:S(2)}) %all-to-all-start.3) | async-done | bytes 2097184 | tf_op jit(solution)/shard_map/all_to_all | solution.py:387
  156.9 7.6 %all-to-all-start.4 = ((bf16[32,48,128]{2,1,0:T(8,128)(2,1)}), bf16[32,48,128]{2,1,0:T(8,128)(2,1)S(1)}, u32[]{:S(2)}, u32[]{:S(2)}) async-start(bf16[32,48,128]{2,1,0:T(8,128)(2,1)} %get-tuple-element.22), calls=%async_computation.4 | async-start | bytes 786432 | tf_op jit(solution)/shard_map/all_to_all | solution.py:398
  164.5 0.9 copy.27
  165.5 10.5 %all-to-all-done.4.late_ref = bf16[32,48,128]{2,1,0:T(8,128)(2,1)S(1)} async-done(((bf16[32,48,128]{2,1,0:T(8,128)(2,1)}), bf16[32,48,128]{2,1,0:T(8,128)(2,1)S(1)}, u32[]{:S(2)}, u32[]{:S(2)}) %all-to-all-start.4) | async-done | bytes 393248 | tf_op jit(solution)/shard_map/all_to_all | solution.py:398
  175.9 3.1 %join.1 = bf16[32,2,128,128]{3,2,1,0:T(8,128)(2,1)} custom-call(bf16[32,2,128,128]{3,2,1,0:T(8,128)(2,1)S(1)} %all-to-all-done.3.old_ref, bf16[32,48,128]{2,1,0:T(8,128)(2,1)S(1)} %all-to-all-done.4.late_ref), custom_call_target="tpu_custom_call" | custom-call | flops 301989888 | bytes 5242880 | tf_op jit(solution)/shard_map/join/pallas_call | solution.py:307
  (28 shorter events, 0.1 us)
Async XLA Ops:
  25.6 15.6 %collective-permute-start.1 = (bf16[2,128,1280]{2,1,0:T(8,128)(2,1)S(1)}, bf16[2,128,1280]{2,1,0:T(8,128)(2,1)S(1)}, u32[]{:S(2)}, u32[]{:S(2)}) collective-permute-start(bf16[2,128,1280]{2,1,0:T(8,128)(2,1)S(1)} %get-tuple-element.24), channel_id=1, source_target_pairs={{0,4},{4,1},{1,5},{5,0},{2,6},{6,3},{3,7},{7,2},{8,12},{12,9},{9,1... | collective-permute-start | bytes 1966088 | tf_op jit(solution)/shard_map/ppermute | solution.py:368
  26.9 17.4 %copy-start.6 = (f32[2,40,512]{2,1,0:T(8,128)S(1)}, f32[2,40,512]{2,1,0:T(8,128)}, u32[]{:S(2)}) copy-start(f32[2,40,512]{2,1,0:T(8,128)} %master_ref.1) | copy-start | bytes 491524
  26.9 17.4 %copy-start.7 = (f32[2,40,512]{2,1,0:T(8,128)S(1)}, f32[2,40,512]{2,1,0:T(8,128)}, u32[]{:S(2)}) copy-start(f32[2,40,512]{2,1,0:T(8,128)} %grad_ref.1) | copy-start | bytes 491524
  26.9 17.4 %copy-start.8 = (f32[2,40,512]{2,1,0:T(8,128)S(1)}, f32[2,40,512]{2,1,0:T(8,128)}, u32[]{:S(2)}) copy-start(f32[2,40,512]{2,1,0:T(8,128)} %first_ref.1) | copy-start | bytes 491524
  26.9 17.4 %copy-start.9 = (f32[2,40,512]{2,1,0:T(8,128)S(1)}, f32[2,40,512]{2,1,0:T(8,128)}, u32[]{:S(2)}) copy-start(f32[2,40,512]{2,1,0:T(8,128)} %second_ref.1) | copy-start | bytes 491524
  26.9 14.4 %collective-permute-start.2 = (bf16[2,128,1280]{2,1,0:T(8,128)(2,1)S(1)}, bf16[2,128,1280]{2,1,0:T(8,128)(2,1)S(1)}, u32[]{:S(2)}, u32[]{:S(2)}) collective-permute-start(bf16[2,128,1280]{2,1,0:T(8,128)(2,1)S(1)} %get-tuple-element.23), channel_id=1, source_target_pairs={{0,5},{4,0},{1,4},{5,1},{2,7},{6,2},{3,6},{7,3},{8,13},{12,8},{9,1... | collective-permute-start | bytes 1966088 | tf_op jit(solution)/shard_map/ppermute | solution.py:369
  28.5 46.8 %collective-permute-start = (bf16[4,128,1280]{2,1,0:T(8,128)(2,1)S(1)}, bf16[4,128,1280]{2,1,0:T(8,128)(2,1)}, u32[]{:S(2)}, u32[]{:S(2)}) collective-permute-start(bf16[4,128,1280]{2,1,0:T(8,128)(2,1)S(1)} %all_to_all.25.x0), channel_id=1, source_target_pairs={{0,2},{2,0},{1,3},{3,1},{4,6},{6,4},{5,7},{7,5},{8,10},{10,8},{9,1... | collective-permute-start | bytes 3932168 | tf_op jit(solution)/shard_map/ppermute | solution.py:373
  41.4 33.9 %collective-permute-start.3 = (bf16[4,128,1280]{2,1,0:T(8,128)(2,1)S(1)}, bf16[4,128,1280]{2,1,0:T(8,128)(2,1)}, u32[]{:S(2)}, u32[]{:S(2)}) collective-permute-start(bf16[4,128,1280]{2,1,0:T(8,128)(2,1)S(1)} %constant_dynamic-update-slice_fusion.x2), channel_id=1, source_target_pairs={{0,2},{2,0},{1,3},{3,1},{4,6},{6,4},{5,7},{7,5},{8,10},{10,8},{9,1... | collective-permute-start | bytes 3932168 | tf_op jit(solution)/shard_map/ppermute | solution.py:374
  45.2 0.8 copy-start.5
  46.0 29.3 %all-to-all-start = ((bf16[32,40,256]{2,1,0:T(8,128)(2,1)}), bf16[32,40,256]{2,1,0:T(8,128)(2,1)S(1)}, u32[]{:S(2)}, u32[]{:S(2)}) async-start(bf16[32,40,256]{2,1,0:T(8,128)(2,1)} %bitcast.24), calls=%async_computation | async-start | bytes 1310720 | tf_op jit(solution)/shard_map/all_to_all | solution.py:357
  79.1 1.0 copy-start
  80.1 4.9 %copy-start.10 = (s32[32]{0:T(128)S(1)}, s32[32]{0:T(128)}, u32[]{:S(2)}) copy-start(s32[32]{0:T(128)} %dest.3) | copy-start | bytes 388
  80.1 5.1 %copy-start.2 = (bf16[32,4,32,128]{3,2,1,0:T(8,128)(2,1)S(1)}, bf16[32,4,32,128]{3,2,1,0:T(8,128)(2,1)}, u32[]{:S(2)}) copy-start(bf16[32,4,32,128]{3,2,1,0:T(8,128)(2,1)} %param.16) | copy-start | bytes 3145732
  80.2 5.1 %copy-start.11 = (s32[32]{0:T(128)S(1)}, s32[32]{0:T(128)}, u32[]{:S(2)}) copy-start(s32[32]{0:T(128)} %prefix.1) | copy-start | bytes 388
  80.2 23.0 %all-to-all-start.2 = ((bf16[16,128,256]{2,1,0:T(8,128)(2,1)}), bf16[16,128,256]{2,1,0:T(8,128)(2,1)S(1)}, u32[]{:S(2)}, u32[]{:S(2)}) async-start(bf16[16,128,256]{2,1,0:T(8,128)(2,1)} %bitcast.21), calls=%async_computation.2 | async-start | bytes 2097152 | tf_op jit(solution)/shard_map/all_to_all | solution.py:391
  100.9 1.3 copy-start.1
  102.2 1.0 copy-start.3
  103.2 5.8 %copy-start.12 = (s32[32]{0:T(128)S(1)}, s32[32]{0:T(128)}, u32[]{:S(2)}) copy-start(s32[32]{0:T(128)} %lengths.1) | copy-start | bytes 388
  103.2 53.7 %all-to-all-start.3 = ((bf16[32,2,128,128]{3,2,1,0:T(8,128)(2,1)}), bf16[32,2,128,128]{3,2,1,0:T(8,128)(2,1)S(1)}, u32[]{:S(2)}, u32[]{:S(2)}) async-start(bf16[32,2,128,128]{3,2,1,0:T(8,128)(2,1)} %copy-done.1), calls=%async_computation.3 | async-start | bytes 4194304 | tf_op jit(solution)/shard_map/all_to_all | solution.py:387
  109.0 1.2 copy-start.4
  156.9 19.0 %all-to-all-start.4 = ((bf16[32,48,128]{2,1,0:T(8,128)(2,1)}), bf16[32,48,128]{2,1,0:T(8,128)(2,1)S(1)}, u32[]{:S(2)}, u32[]{:S(2)}) async-start(bf16[32,48,128]{2,1,0:T(8,128)(2,1)} %get-tuple-element.22), calls=%async_computation.4 | async-start | bytes 786432 | tf_op jit(solution)/shard_map/all_to_all | solution.py:398

commit v2 on v0

v2 whole, which is shorter than its diff:
```python
import functools
import jax
import jax.numpy as jnp
from jax import lax
from jax.experimental import pallas as pl
from jax.experimental.pallas import tpu as pltpu
from jax.sharding import Mesh, PartitionSpec as P

beta_one = 0.9
beta_two = 0.95
adam_eps = 1e-08
learn_rate = 0.002
weight_decay = 0.1
adam_step = 10.0
rope_theta = 1000000.0
norm_eps = 1e-06
masked_score = -1e30

N_Y = 4
N_Z = 8
N_GEN = 4
N_FSDP = N_Y * N_Z
HEAD = 128
HEADS = 4
STEPS = 4
ROLL = 32
TOKENS = ROLL * STEPS
CACHE = 128
ROWS = 40
DEPTH = 1280
SLOTS = 2
SCALE = HEAD ** (-0.5)
F32 = jnp.float32
BF16 = jnp.bfloat16
VMEM_BYTES = 40 * 1024 * 1024
VMEM_MOST = 60 * 1024 * 1024


SMALL = pl.CostEstimate(flops=1000, bytes_accessed=1000, transcendentals=0)


def params(limit=VMEM_BYTES):
    return pltpu.CompilerParams(vmem_limit_bytes=limit)


def whole():
    return pl.BlockSpec(memory_space=pltpu.VMEM)


def iota(shape, axis):
    return lax.broadcasted_iota(jnp.int32, shape, axis)


def after(value, *others):
    anywhere = pl.BlockSpec(memory_space=pl.ANY)
    return pl.pallas_call(
        lambda *refs: None,
        in_specs=[anywhere] * (1 + len(others)),
        out_specs=anywhere,
        out_shape=jax.ShapeDtypeStruct(value.shape, value.dtype),
        input_output_aliases={0: 0},
        cost_estimate=SMALL,
        name="after",
    )(value, *others)


def adam_kernel(*refs):
    sources, (m_out, f_out, s_out, w_out) = refs[:4], refs[4:8]
    held, sems = refs[8], refs[9]
    copies = [
        pltpu.make_async_copy(source, held.at[i], sems.at[i]) for i, source in enumerate(sources)
    ]
    for copy in copies:
        copy.start()
    for copy in copies:
        copy.wait()
    for kv in range(2):
        master, grad, first, second = (held[i, kv] for i in range(4))
        first = beta_one * first + (1.0 - beta_one) * grad
        second = beta_two * second + (1.0 - beta_two) * grad * grad
        first_hat = first / (1.0 - beta_one**adam_step)
        second_hat = second / (1.0 - beta_two**adam_step)
        master = master - learn_rate * (
            first_hat / (jnp.sqrt(second_hat) + adam_eps) + weight_decay * master
        )
        f_out[kv] = first
        s_out[kv] = second
        m_out[kv] = master
        rounded = master.astype(BF16)
        for q in range(N_GEN):
            piece = rounded[:, q * HEAD : (q + 1) * HEAD]
            for z in range(N_Z):
                w_out[z, q, :, kv * HEAD : (kv + 1) * HEAD] = piece


def adam(master, grad, first, second):
    shape = jax.ShapeDtypeStruct(master.shape, F32)
    return pl.pallas_call(
        adam_kernel,
        out_shape=(shape, shape, shape, jax.ShapeDtypeStruct((N_Z, N_GEN, ROWS, 2 * HEAD), BF16)),
        in_specs=[pl.BlockSpec(memory_space=pl.ANY)] * 4,
        out_specs=(whole(),) * 4,
        scratch_shapes=[
            pltpu.VMEM((4,) + master.shape, F32),
            pltpu.SemaphoreType.DMA((4,)),
        ],
        compiler_params=params(VMEM_MOST),
        cost_estimate=SMALL,
        name="adam",
    )(master, grad, first, second)


def columns_kernel(x_ref, _, out_ref, low_ref, high_ref):
    block = x_ref[...].reshape(TOKENS, DEPTH)
    out_ref[0] = block
    low_ref[0] = block[: TOKENS // 2]
    high_ref[0] = block[TOKENS // 2 :]


def columns(inputs, later):
    def shape(rows):
        return jax.ShapeDtypeStruct((N_Y, rows, DEPTH), BF16)

    def block(rows):
        return pl.BlockSpec((1, rows, DEPTH), lambda i: (i, 0, 0))

    return pl.pallas_call(
        columns_kernel,
        grid=(N_Y,),
        in_specs=[
            pl.BlockSpec((ROLL, STEPS, DEPTH), lambda i: (0, 0, i)),
            pl.BlockSpec(memory_space=pl.ANY),
        ],
        out_specs=(block(TOKENS), block(TOKENS // 2), block(TOKENS // 2)),
        out_shape=(shape(TOKENS), shape(TOKENS // 2), shape(TOKENS // 2)),
        compiler_params=params(),
        cost_estimate=SMALL,
        name="columns",
    )(inputs, later)


OLD_BLOCK = 8
PIECE = TOKENS // N_Y
LOG2E = 1.4426950408889634


def old_kernel(prefix, q_ref, k_ref, v_ref, _, out_ref, lse_ref, qp_ref, bias_ref):
    step = pl.program_id(0)
    span = CACHE * HEADS
    block = range(OLD_BLOCK)

    @pl.when(step == 0)
    def _():
        row, col = iota((TOKENS, span), 0), iota((TOKENS, span), 1)
        bias_ref[...] = jnp.where(col % HEADS == row // 32, 0.0, masked_score)

    row, col = iota((TOKENS, TOKENS), 0), iota((TOKENS, TOKENS), 1)
    perm = ((col % 32 == row // 4) & (col // 32 == row % 4)).astype(BF16)
    lane = iota((1, span), 1)
    query = [
        jnp.dot(perm, q_ref[n], preferred_element_type=F32).astype(BF16) for n in block
    ]
    for n in block:
        qp_ref[n] = query[n]
    score = [
        lax.dot_general(
            query[n], k_ref[n], (((1,), (1,)), ((), ())), preferred_element_type=F32
        )
        for n in block
    ]
    score = [
        score[n]
        + bias_ref[...]
        + jnp.where(lane < prefix[step * OLD_BLOCK + n] * HEADS, 0.0, masked_score)
        for n in block
    ]
    top = [jnp.max(s, axis=1, keepdims=True) for s in score]
    weight = [jnp.exp2((s - t) * (SCALE * LOG2E)) for s, t in zip(score, top)]
    total = [jnp.sum(w, axis=1, keepdims=True) for w in weight]
    mixed = [
        jnp.dot(weight[n].astype(BF16), v_ref[n], preferred_element_type=F32) for n in block
    ]
    for n in block:
        out_ref[n] = mixed[n] * (1.0 / total[n])
        lse_ref[n] = jnp.broadcast_to(top[n] * SCALE + jnp.log(total[n]), (TOKENS, HEAD))


def old_attention(prefix, queries, keys, values, later):
    span = CACHE * HEADS
    inside = pl.BlockSpec((OLD_BLOCK, TOKENS, HEAD), lambda i, *_: (i, 0, 0))
    cache = pl.BlockSpec((OLD_BLOCK, span, HEAD), lambda i, *_: (i, 0, 0))
    rows = (ROLL, TOKENS, HEAD)
    return pl.pallas_call(
        old_kernel,
        grid_spec=pltpu.PrefetchScalarGridSpec(
            num_scalar_prefetch=1,
            grid=(ROLL // OLD_BLOCK,),
            in_specs=[inside, cache, cache, pl.BlockSpec(memory_space=pl.ANY)],
            out_specs=(inside, inside, inside),
            scratch_shapes=[pltpu.VMEM((TOKENS, span), F32)],
        ),
        out_shape=(
            jax.ShapeDtypeStruct(rows, F32),
            jax.ShapeDtypeStruct(rows, F32),
            jax.ShapeDtypeStruct(rows, BF16),
        ),
        compiler_params=params(VMEM_MOST),
        cost_estimate=SMALL,
        name="old_attention",
    )(prefix, queries, keys, values, later)


def halves_kernel(before, beyond, _, low, high):
    half = DEPTH // 2
    low[...] = before[:half]
    high[...] = beyond[half:]


def halves(before, beyond, later):
    shape = jax.ShapeDtypeStruct((DEPTH // 2, 2 * HEAD), BF16)
    return pl.pallas_call(
        halves_kernel,
        in_specs=[whole(), whole(), pl.BlockSpec(memory_space=pl.ANY)],
        out_specs=(whole(),) * 2,
        out_shape=(shape,) * 2,
        compiler_params=params(),
        cost_estimate=SMALL,
        name="halves",
    )(before, beyond, later)


def project_kernel(shifts, sources, carried, last, me, *refs):
    weights, refs = refs[: len(shifts)], refs[len(shifts) :]
    own, near, *far = refs[: 2 if sources == 2 else 6]
    out_ref = refs[-1]
    half = TOKENS // 2
    places = [(own, 0, 0, TOKENS), (near, 1, 0, TOKENS)]
    for n, ref in enumerate(far):
        places.append((ref, 2 + n // 2, n % 2 * half, n % 2 * half + half))
    for ref, j, start, stop in places:
        total = refs[-2][j, start:stop] if j < carried else None
        at = 0
        for n, (shift, weight) in enumerate(zip(shifts, weights)):
            if n == 0 and j < carried and shift == 0:
                continue
            part = (me[0] + (N_Y - shift)) % N_Y
            depth = weight.shape[0]
            term = jnp.dot(ref[part, :, at : at + depth], weight[...], preferred_element_type=F32)
            total = term if total is None else total + term
            at = (at + depth) % DEPTH
        if last:
            key, value = total[:, :HEAD], total[:, HEAD:]
            high = key.astype(BF16)
            out_ref[j, start:stop, :HEAD] = high
            out_ref[j, start:stop, HEAD : 2 * HEAD] = (key - high.astype(F32)).astype(BF16)
            out_ref[j, start:stop, 2 * HEAD :] = value.astype(BF16)
        else:
            out_ref[j, start:stop] = total


def project(me, shifts, weights, inputs, total, last):
    width, dtype = (3 * HEAD, BF16) if last else (2 * HEAD, F32)
    sources = 2 if len(inputs) == 2 else N_GEN
    carried = () if total is None else (total,)
    return pl.pallas_call(
        functools.partial(
            project_kernel, shifts, sources, 0 if total is None else total.shape[0], last
        ),
        in_specs=[pl.BlockSpec(memory_space=pltpu.SMEM)]
        + [whole()] * (len(weights) + len(inputs) + len(carried)),
        out_specs=whole(),
        out_shape=jax.ShapeDtypeStruct((sources, TOKENS, width), dtype),
        compiler_params=params(),
        cost_estimate=SMALL,
        name="project",
    )(me, *weights, *inputs, *carried)


FRESH_BLOCK = 16
QUAD = 4


def fresh_kernel(
    dest, slot, lengths, me, p0, p1, p2, p3, cos_ref, sin_ref, qp_ref, lse_ref, old_ref,
    kv_ref, out_ref,
):
    step = pl.program_id(0)

    @pl.when(step == 0)
    def _():
        cosine, sine = cos_ref[...], sin_ref[...]
        for j, part in enumerate((p0, p1, p2, p3)):
            g = me[1] ^ j
            key = part[:, :HEAD].astype(F32) + part[:, HEAD : 2 * HEAD].astype(F32)
            key = key / jnp.sqrt(jnp.mean(key * key, axis=-1, keepdims=True) + norm_eps)
            key = key * cosine + pltpu.roll(key, HEAD // 2, 1) * sine
            kv_ref[0, g] = key.astype(BF16)
            kv_ref[1, g] = part[:, 2 * HEAD :]
        out_ref[...] = jnp.zeros_like(out_ref)

    wide = QUAD * STEPS * HEADS
    row, col = iota((QUAD * TOKENS, wide), 0), iota((QUAD * TOKENS, wide), 1)
    own = (
        (row // TOKENS == (col % 16) // STEPS)
        & (row % TOKENS // 32 == col // 16)
        & (col % STEPS <= row % STEPS)
    )
    tall = iota((QUAD * TOKENS, 1), 0)
    groups = range(FRESH_BLOCK // QUAD)
    fresh = [
        [
            jnp.concatenate(
                [
                    kv_ref[
                        kind,
                        g,
                        pl.ds(pl.multiple_of((step * len(groups) + n) * 16, 16), 16),
                    ]
                    for g in range(HEADS)
                ],
                axis=0,
            )
            for n in groups
        ]
        for kind in range(2)
    ]

    def rows(ref, n):
        return ref[n * QUAD : (n + 1) * QUAD].reshape(QUAD * TOKENS, HEAD)

    score = [
        lax.dot_general(
            rows(qp_ref, n), fresh[0][n], (((1,), (1,)), ((), ())), preferred_element_type=F32
        )
        for n in groups
    ]
    score = [jnp.where(own, s * SCALE, masked_score) for s in score]
    lse = [rows(lse_ref, n)[:, :1] for n in groups]
    top = [jnp.maximum(jnp.max(s, axis=1, keepdims=True), old) for s, old in zip(score, lse)]
    weight = [jnp.exp(s - t) for s, t in zip(score, top)]
    share = [jnp.exp(old - t) for old, t in zip(lse, top)]
    total = [jnp.sum(w, axis=1, keepdims=True) + a for w, a in zip(weight, share)]
    for n in groups:
        first = step * FRESH_BLOCK + n * QUAD
        length = lengths[first]
        for k in range(1, QUAD):
            length = jnp.where(tall < k * TOKENS, length, lengths[first + k])
        kept = (tall % STEPS) < length
        scale = jnp.where(kept, 1.0 / total[n], 0.0)
        mixed = (share[n] * scale) * rows(old_ref, n) + jnp.dot(
            (weight[n] * scale).astype(BF16), fresh[1][n], preferred_element_type=F32
        )
        mixed = mixed.astype(BF16)
        for k in range(QUAD):
            out_ref[dest[first + k], slot[first + k]] = mixed[k * TOKENS : (k + 1) * TOKENS]


def fresh(dest, slot, lengths, me, parts, cosine, sine, queries, lse, old):
    def whole_block(shape):
        return pl.BlockSpec(shape, lambda i, *_: (0,) * len(shape))

    inside = pl.BlockSpec((FRESH_BLOCK, TOKENS, HEAD), lambda i, *_: (i, 0, 0))
    kv = (2, HEADS, TOKENS, HEAD)
    out = (N_FSDP, SLOTS, TOKENS, HEAD)
    return pl.pallas_call(
        fresh_kernel,
        grid_spec=pltpu.PrefetchScalarGridSpec(
            num_scalar_prefetch=4,
            grid=(ROLL // FRESH_BLOCK,),
            in_specs=[whole_block((TOKENS, 3 * HEAD))] * 4
            + [whole_block((TOKENS, HEAD))] * 2
            + [inside] * 3,
            out_specs=(whole_block(kv), whole_block(out)),
        ),
        out_shape=(jax.ShapeDtypeStruct(kv, BF16), jax.ShapeDtypeStruct(out, BF16)),
        compiler_params=params(),
        cost_estimate=SMALL,
        name="fresh",
    )(dest, slot, lengths, me, *parts, cosine, sine, queries, lse, old)


def in_rows(joined):
    joined = joined.reshape(N_FSDP, SLOTS, 8 * HEADS, STEPS, HEAD).transpose(0, 1, 3, 2, 4)
    return joined.reshape(1, 1, N_FSDP, SLOTS, STEPS, 8 * HEADS * HEAD)


def turn_tables(prefix_lengths):
    half_size = HEAD // 2
    exponent = -2.0 * jnp.arange(half_size).astype(F32) / HEAD
    inverse_freq = jnp.power(jnp.float32(rope_theta), exponent)
    positions = prefix_lengths[:, None] + jnp.arange(STEPS, dtype=jnp.int32)[None, :]
    angle = positions.reshape(TOKENS, 1).astype(F32) * inverse_freq
    cosine, sine = jnp.cos(angle), jnp.sin(angle)
    return (
        jnp.concatenate([cosine, cosine], axis=-1),
        jnp.concatenate([-sine, sine], axis=-1),
    )


def along(moves):
    def place_of(x):
        return (x % 2) * 2 + x // 2

    return [(place_of(start), place_of(stop)) for start, stop in moves]


def shift_y(k):
    return [(y, (y + k) % N_Y) for y in range(N_Y)]


def on_device(
    master_weight,
    gradient,
    first_moment,
    second_moment,
    new_inputs,
    queries,
    cache_keys,
    cache_values,
    prefix_lengths,
    rollout_lengths,
    destinations,
):
    new_master, new_first, new_second, blocks = adam(
        master_weight, gradient, first_moment, second_moment
    )
    own_rows = lax.all_to_all(
        blocks.reshape(N_Z * N_GEN, ROWS, 2 * HEAD), ("z", "xl", "c"), 0, 0, tiled=True
    ).reshape(DEPTH, 2 * HEAD)

    core = [(0, 1), (1, 0)]
    own, low, high = columns(new_inputs, blocks)
    right = [(x, (x + 1) % 4) for x in range(4)]
    left = [(x, (x + 3) % 4) for x in range(4)]
    near = lax.ppermute(own, "c", core)
    far_a = lax.ppermute(low, ("xl", "tp"), along(right))
    far_b = lax.ppermute(high, ("xl", "tp"), along(left))
    both_a, both_b = (lax.ppermute(far, "c", core) for far in (far_a, far_b))
    inputs = (own, near, far_a, far_b, both_a, both_b)

    same_dest = destinations[:, None] == destinations[None, :]
    earlier = jnp.arange(ROLL)[None, :] < jnp.arange(ROLL)[:, None]
    slot_rank = jnp.sum((same_dest & earlier).astype(jnp.int32), axis=1)
    old_rows, lse, ordered = old_attention(
        prefix_lengths,
        queries.reshape(ROLL, TOKENS, HEAD),
        cache_keys.reshape(ROLL, CACHE * HEADS, HEAD),
        cache_values.reshape(ROLL, CACHE * HEADS, HEAD),
        own,
    )
    own_rows = after(own_rows, lse)
    me = jnp.stack([lax.axis_index("y"), lax.axis_index("xl") * 2 + lax.axis_index("c")])
    before = lax.ppermute(own_rows, "y", shift_y(1))
    beyond = lax.ppermute(own_rows, "y", shift_y(-1))
    total = project(me, (0,), (own_rows,), inputs[:2], None, False)
    low, high = halves(before, beyond, total)
    across = [lax.ppermute(low, "y", shift_y(1)), lax.ppermute(high, "y", shift_y(-1))]
    total = project(me, (0, 1, 3), (own_rows, before, beyond), inputs, total, False)
    parts = project(me, (2, 2), across, inputs, total, True)
    parts = [parts[0]] + [
        lax.ppermute(parts[j], ("xl", "c"), [(q, q ^ j) for q in range(N_GEN)]) for j in (1, 2, 3)
    ]
    cosine, sine = turn_tables(prefix_lengths)
    fresh_parts, rows = fresh(
        destinations, slot_rank, rollout_lengths, me, parts, cosine, sine, ordered, lse, old_rows
    )
    rows = lax.all_to_all(rows, ("y", "z"), 0, 0, tiled=True)
    fresh_kv = fresh_parts.reshape(2, HEADS, ROLL, STEPS, HEAD).transpose(2, 3, 0, 1, 4)
    returned_rows = in_rows(rows)
    return (new_master, new_first, new_second, fresh_kv, returned_rows)


def solution(mesh):
    fine = Mesh(mesh.devices.reshape(N_Y, N_Z, 2, 2, 2), ("y", "z", "xl", "c", "tp"))
    group = ("y", "z", "xl", "c")
    rows = P(None, group, "tp")
    in_specs = (
        rows,
        rows,
        rows,
        rows,
        P(group, None, None),
        P(group, None, "tp", None),
        P(group, None, "tp", None),
        P(group, None, "tp", None),
        P(group),
        P(group),
        P(group),
    )
    out_specs = (
        rows,
        rows,
        rows,
        P(group, None, None, "tp", None),
        P(("y", "z"), ("xl", "c"), None, None, None, "tp"),
    )
    return jax.shard_map(
        on_device, mesh=fine, in_specs=in_specs, out_specs=out_specs, check_vma=False
    )
```

time: 340 us -> 136 us (0.40)
  waiting for transfers between devices: 264 us -> 67.1 us
  Pallas kernels: 0 us -> 28.2 us
  starting transfers between devices: 6.14 us -> 33.4 us
  matrix products: 24.6 us -> 0 us
  other arithmetic: 14.3 us -> 0.74 us
  between operations: 14.3 us -> 0.84 us
  local copies, waits for them, and re-layouts: 14 us -> 5.44 us
    all_gather x1 -> x0, waiting for transfers between devices: 218 us -> none  [on_device(): lax.all_gather(weight_bf, ('fsdp', 'gen'), axis=1, tiled=True)]
    pallas_call x0 -> x9, Pallas kernels: none -> 28.2 us  [the longest x1 9.02 us: old_attention(): pl.pallas_call(old_kernel, grid_spec=pltpu.PrefetchScalarGridSpec(num_sca...]
    dot_general x7 -> x0, matrix products: 24.6 us -> none  [the longest x1 5.46 us: on_device(): jnp.einsum('rsgqh,rtgh->rgqst', grouped, fresh_keys, preferred_element_ty...]
    ppermute x0 -> x12, starting transfers between devices: none -> 16 us  [the longest x3 5.91 us: on_device(): lax.ppermute(parts[j], ('xl', 'c'), [(q, q ^ j) for q in range(N_GEN)])]
    ppermute x0 -> x12, waiting for transfers between devices: none -> 14 us  [the longest x1 6.71 us: on_device(): before = lax.ppermute(own_rows, 'y', shift_y(1))]
    all_to_all x1 -> x2, starting transfers between devices: 6.1 us -> 17.5 us  [the longest x1 11.1 us: on_device(): lax.all_to_all(blocks.reshape(N_Z * N_GEN, ROWS, 2 * HEAD), ('z', 'xl', '...]
    all_to_all x1 -> x2, waiting for transfers between devices: 45.9 us -> 53.1 us  [the longest x1 48.8 us: on_device(): rows = lax.all_to_all(rows, ('y', 'z'), 0, 0, tiled=True)]
    convert_element_type x6 -> x1, local copies, waits for them, and re-layouts: 5.58 us -> 0.11 us  [turn_tables(): angle = positions.reshape(TOKENS, 1).astype(F32) * inverse_freq]
  transfers between devices with their start and end apart: 2 -> 14, of which waited for: 2 -> 7; matrix products, arithmetic and copies ran while one was open for 4% -> 1% of each run, Pallas kernels for 0% -> 12%
where the time goes in v2:
time: 136 us
  waiting for transfers between devices  67.1 us (49%)
  starting transfers between devices  33.4 us (25%)
  Pallas kernels  28.2 us (21%)
  local copies, waits for them, and re-layouts  5.44 us (4%)
    all_to_all x1, waiting for transfers between devices, on_device(): rows = lax.all_to_all(rows, ('y', 'z'), 0, 0, tiled=True)  48.8 us
    all_to_all x1, starting transfers between devices, on_device(): lax.all_to_all(blocks.reshape(N_Z * N_GEN, ROWS, 2 * HEAD), ('z', 'xl', '...  11.1 us
    pallas_call x1, Pallas kernels, old_attention(): pl.pallas_call(old_kernel, grid_spec=pltpu.PrefetchScalarGridSpec(num_sca...  9.02 us
    pallas_call x3, Pallas kernels, project(): pl.pallas_call(functools.partial(project_kernel, shifts, sources, 0 if to...  8.26 us
    ppermute x1, waiting for transfers between devices, on_device(): before = lax.ppermute(own_rows, 'y', shift_y(1))  6.71 us
    all_to_all x1, starting transfers between devices, on_device(): rows = lax.all_to_all(rows, ('y', 'z'), 0, 0, tiled=True)  6.39 us
    pallas_call x1, Pallas kernels, fresh(): pl.pallas_call(fresh_kernel, grid_spec=pltpu.PrefetchScalarGridSpec(num_s...  6.25 us
    ppermute x3, starting transfers between devices, on_device(): lax.ppermute(parts[j], ('xl', 'c'), [(q, q ^ j) for q in range(N_GEN)])  5.91 us
  transfers between devices with their start and end apart: 14, of which 7 were waited for; matrix products, arithmetic and copies ran while one was open for 1% of the time, Pallas kernels for 12%

profile of v2, /device:TPU:1, one launch (start us, length us, event | category | flops | bytes accessed | tf_op | source)
XLA Modules:
  0.0 135.7 jit_solution(15942868980075913903)
XLA Ops:
  0.6 2.4 %adam.1 = (f32[2,40,512]{2,1,0:T(8,128)}, f32[2,40,512]{2,1,0:T(8,128)}, f32[2,40,512]{2,1,0:T(8,128)}, bf16[8,4,40,256]{3,2,1,0:T(8,128)(2,1)}) custom-call(f32[2,40,512]{2,1,0:T(8,128)} %refs_0_.1, f32[2,40,512]{2,1,0:T(8,128)} %refs_1_.1, f32[2,40,512]{2,1,0:T(8,128)} %refs_2_.1, f32[2,40,512]{2,1,0:T(8,128)} %refs_3_.1), custom_call_target="tpu_custom_call" | custom-call | flops 1000 | bytes 1000 | tf_op jit(solution)/shard_map/adam/pallas_call | solution.py:98
  3.0 11.1 %all-to-all-start = ((bf16[32,40,256]{2,1,0:T(8,128)(2,1)}), bf16[32,40,256]{2,1,0:T(8,128)(2,1)S(1)}, u32[]{:S(2)}, u32[]{:S(2)}) async-start(bf16[32,40,256]{2,1,0:T(8,128)(2,1)} %bitcast.25), calls=%async_computation | async-start | bytes 1310720 | tf_op jit(solution)/shard_map/all_to_all | solution.py:427
  14.1 1.1 copy-done.4
  15.2 2.2 %columns.1 = (bf16[4,128,1280]{2,1,0:T(8,128)(2,1)}, bf16[4,64,1280]{2,1,0:T(8,128)(2,1)}, bf16[4,64,1280]{2,1,0:T(8,128)(2,1)}) custom-call(bf16[32,4,5120]{2,1,0:T(4,128)(2,1)S(1)} %copy-done.6, bf16[8,4,40,256]{3,2,1,0:T(8,128)(2,1)S(1)} %copy-done.4), custom_call_target="tpu_custom_call" | custom-call | flops 1000 | bytes 1000 | tf_op jit(solution)/shard_map/columns/pallas_call | solution.py:127
  17.7 1.5 %collective-permute-start.5 = (bf16[4,64,1280]{2,1,0:T(8,128)(2,1)}, bf16[4,64,1280]{2,1,0:T(8,128)(2,1)S(1)}, u32[]{:S(2)}, u32[]{:S(2)}) collective-permute-start(bf16[4,64,1280]{2,1,0:T(8,128)(2,1)} %get-tuple-element.27), channel_id=1, source_target_pairs={{0,4},{4,1},{1,5},{5,0},{2,6},{6,3},{3,7},{7,2},{8,12},{12,9},{9,1... | collective-permute-start | bytes 1966088 | tf_op jit(solution)/shard_map/ppermute | solution.py:436
  19.2 1.3 collective-permute-start.6
  20.5 9.0 %old_attention.1 = (f32[32,128,128]{2,1,0:T(8,128)}, f32[32,128,128]{2,1,0:T(8,128)}, bf16[32,128,128]{2,1,0:T(8,128)(2,1)}) custom-call(s32[32]{0:T(128)} %prefix.1, bf16[32,128,128]{2,1,0:T(8,128)(2,1)} %bitcast.30, bf16[32,512,128]{2,1,0:T(8,128)(2,1)} %bitcast.28, bf16[32,512,128]{2,1,0:T(8,128)(2,1)} %bitcast.29, ...), custom_call_target="tpu_custom_call" | custom-call | flops 1000 | bytes 1000 | tf_op jit(solution)/shard_map/old_attention/pallas_call | solution.py:193
  29.5 4.3 %all-to-all-done = bf16[32,40,256]{2,1,0:T(8,128)(2,1)S(1)} async-done(((bf16[32,40,256]{2,1,0:T(8,128)(2,1)}), bf16[32,40,256]{2,1,0:T(8,128)(2,1)S(1)}, u32[]{:S(2)}, u32[]{:S(2)}) %all-to-all-start) | async-done | bytes 655392 | tf_op jit(solution)/shard_map/all_to_all | solution.py:427
  33.7 0.8 copy-done
  34.6 1.3 collective-permute-start
  35.9 1.4 %collective-permute-start.1 = (bf16[1280,256]{1,0:T(8,128)(2,1)}, bf16[1280,256]{1,0:T(8,128)(2,1)S(1)}, u32[]{:S(2)}, u32[]{:S(2)}) collective-permute-start(bf16[1280,256]{1,0:T(8,128)(2,1)} %after.1.refs_0_), channel_id=1, source_target_pairs={{0,192},{64,0},{128,64},{192,128},{1,193},{65,1},{129,65},{193,129... | collective-permute-start | bytes 1966088 | tf_op jit(solution)/shard_map/ppermute | solution.py:454
  37.3 1.0 collective-permute-done.5.refs_5_.refs_4_
  38.3 0.8 collective-permute-start.7
  39.2 1.3 collective-permute-done.6.refs_6_.refs_5_
  40.4 0.7 collective-permute-start.8
  41.5 1.1 copy-done.1
  42.5 1.7 %project.3._.refs_9_ = f32[2,128,256]{2,1,0:T(8,128)S(1)} custom-call(s32[2]{0:T(128)S(1)} %pad_add_fusion.me, bf16[1280,256]{1,0:T(8,128)(2,1)S(1)} %copy-done.1, bf16[4,128,1280]{2,1,0:T(8,128)(2,1)} %get-tuple-element.23._.refs_1_.refs_3_.refs_2_, bf16[4,128,1280]{2,1,0:T(8,128)(2,1)S(1)} %collective-permute-done.2.refs_2_.refs_4_.refs_3_), custom_call_target="tpu_custom_call" | custom-call | flops 1000 | bytes 1000 | tf_op jit(solution)/shard_map/project/pallas_call | solution.py:265
  44.3 6.7 %collective-permute-done.before.refs_1_ = bf16[1280,256]{1,0:T(8,128)(2,1)S(1)} collective-permute-done((bf16[1280,256]{1,0:T(8,128)(2,1)}, bf16[1280,256]{1,0:T(8,128)(2,1)S(1)}, u32[]{:S(2)}, u32[]{:S(2)}) %collective-permute-start) | collective-permute-done | bytes 655392 | tf_op jit(solution)/shard_map/ppermute | solution.py:453
  51.0 1.1 collective-permute-start.3
  52.1 1.7 %collective-permute-start.4 = (bf16[640,256]{1,0:T(8,128)(2,1)S(1)}, bf16[640,256]{1,0:T(8,128)(2,1)S(1)}, u32[]{:S(2)}, u32[]{:S(2)}) collective-permute-start(bf16[640,256]{1,0:T(8,128)(2,1)S(1)} %get-tuple-element.26), channel_id=1, source_target_pairs={{0,192},{64,0},{128,64},{192,128},{1,193},{65,1},{129,65},{193,129... | collective-permute-start | bytes 983048 | tf_op jit(solution)/shard_map/ppermute | solution.py:457
  53.8 0.3 fusion
  54.2 3.7 %project.4.refs_8_ = f32[4,128,256]{2,1,0:T(8,128)S(1)} custom-call(s32[2]{0:T(128)S(1)} %pad_add_fusion.me, bf16[1280,256]{1,0:T(8,128)(2,1)S(1)} %copy-done.2, bf16[1280,256]{1,0:T(8,128)(2,1)S(1)} %collective-permute-done.before.refs_1_, bf16[1280,256]{1,0:T(8,128)(2,1)S(1)} %collective-permute-done.1.beyond.refs_2_, ...), custom_call_target="tpu_custom_call" | custom-call | flops 1000 | bytes 1000 | tf_op jit(solution)/shard_map/project/pallas_call | solution.py:265
  58.0 1.3 collective-permute-done.3.refs_0_
  59.3 2.8 %project.5 = bf16[4,128,384]{2,1,0:T(8,128)(2,1)S(1)} custom-call(s32[2]{0:T(128)S(1)} %pad_add_fusion.me, bf16[640,256]{1,0:T(8,128)(2,1)S(1)} %collective-permute-done.3.refs_0_, bf16[640,256]{1,0:T(8,128)(2,1)S(1)} %collective-permute-done.4.refs_1_, bf16[4,128,1280]{2,1,0:T(8,128)(2,1)} %get-tuple-element.23._.refs_1_.refs_3_.refs_2_, ...), custom_call_target="tpu_custom_call" | custom-call | flops 1000 | bytes 1000 | tf_op jit(solution)/shard_map/project/pallas_call | solution.py:265
  62.2 3.0 %collective-permute-start.10 = (bf16[128,384]{1,0:T(8,128)(2,1)S(1)}, bf16[128,384]{1,0:T(8,128)(2,1)S(1)}, u32[]{:S(2)}, u32[]{:S(2)}) collective-permute-start(bf16[128,384]{1,0:T(8,128)(2,1)S(1)} %get-tuple-element.34), channel_id=1, source_target_pairs={{0,4},{2,6},{4,0},{6,2},{1,5},{3,7},{5,1},{7,3},{8,12},{10,14},{12... | collective-permute-start | bytes 294920 | tf_op jit(solution)/shard_map/ppermute | solution.py:461
  65.2 2.6 %collective-permute-start.11 = (bf16[128,384]{1,0:T(8,128)(2,1)S(1)}, bf16[128,384]{1,0:T(8,128)(2,1)S(1)}, u32[]{:S(2)}, u32[]{:S(2)}) collective-permute-start(bf16[128,384]{1,0:T(8,128)(2,1)S(1)} %get-tuple-element.33), channel_id=1, source_target_pairs={{0,6},{2,4},{4,2},{6,0},{1,7},{3,5},{5,3},{7,1},{8,14},{10,12},{12... | collective-permute-start | bytes 294920 | tf_op jit(solution)/shard_map/ppermute | solution.py:461
  68.3 3.7 %collective-permute-done.11.p3 = bf16[128,384]{1,0:T(8,128)(2,1)S(1)} collective-permute-done((bf16[128,384]{1,0:T(8,128)(2,1)S(1)}, bf16[128,384]{1,0:T(8,128)(2,1)S(1)}, u32[]{:S(2)}, u32[]{:S(2)}) %collective-permute-start.11) | collective-permute-done | bytes 98336 | tf_op jit(solution)/shard_map/ppermute | solution.py:461
  72.0 6.2 %fresh.1 = (bf16[2,4,128,128]{3,2,1,0:T(8,128)(2,1)S(1)}, bf16[32,2,128,128]{3,2,1,0:T(8,128)(2,1)}) custom-call(s32[32]{0:T(128)S(1)} %copy-done.8, s32[32]{0:T(128)S(1)} %convert_reduce_fusion.slot, s32[32]{0:T(128)S(1)} %copy-done.9, s32[2]{0:T(128)S(1)} %pad_add_fusion.me, bf16[128,384]{1,0:T(8,128)(2,1)S(1)} %get-tuple-element.36.p0, ...), custom_call_target="tpu_custom_call" | custom-call | flops 1000 | bytes 1000 | tf_op jit(solution)/shard_map/fresh/pallas_call | solution.py:365
  78.2 6.4 %all-to-all-start.1 = ((bf16[32,2,128,128]{3,2,1,0:T(8,128)(2,1)}), bf16[32,2,128,128]{3,2,1,0:T(8,128)(2,1)S(1)}, u32[]{:S(2)}, u32[]{:S(2)}) async-start(bf16[32,2,128,128]{3,2,1,0:T(8,128)(2,1)} %get-tuple-element.32), calls=%async_computation.1 | async-start | bytes 4194304 | tf_op jit(solution)/shard_map/all_to_all | solution.py:467
  84.6 0.9 copy.24
  85.5 48.8 %all-to-all-done.1 = bf16[32,2,128,128]{3,2,1,0:T(8,128)(2,1)S(1)} async-done(((bf16[32,2,128,128]{3,2,1,0:T(8,128)(2,1)}), bf16[32,2,128,128]{3,2,1,0:T(8,128)(2,1)S(1)}, u32[]{:S(2)}, u32[]{:S(2)}) %all-to-all-start.1) | async-done | bytes 2097184 | tf_op jit(solution)/shard_map/all_to_all | solution.py:467
  134.4 1.3 copy.27
  (37 shorter events, 1.2 us)
Async XLA Ops:
  0.6 13.5 %copy-start.6 = (bf16[32,4,5120]{2,1,0:T(4,128)(2,1)S(1)}, bf16[32,4,5120]{2,1,0:T(4,128)(2,1)}, u32[]{:S(2)}) copy-start(bf16[32,4,5120]{2,1,0:T(4,128)(2,1)} %x_ref.1) | copy-start | bytes 3932164
  3.0 30.7 %all-to-all-start = ((bf16[32,40,256]{2,1,0:T(8,128)(2,1)}), bf16[32,40,256]{2,1,0:T(8,128)(2,1)S(1)}, u32[]{:S(2)}, u32[]{:S(2)}) async-start(bf16[32,40,256]{2,1,0:T(8,128)(2,1)} %bitcast.25), calls=%async_computation | async-start | bytes 1310720 | tf_op jit(solution)/shard_map/all_to_all | solution.py:427
  14.1 1.1 copy-start.4
  17.4 24.0 %collective-permute-start.2 = (bf16[4,128,1280]{2,1,0:T(8,128)(2,1)}, bf16[4,128,1280]{2,1,0:T(8,128)(2,1)S(1)}, u32[]{:S(2)}, u32[]{:S(2)}) collective-permute-start(bf16[4,128,1280]{2,1,0:T(8,128)(2,1)} %get-tuple-element.23._.refs_1_.refs_3_.refs_2_), channel_id=1, source_target_pairs={{0,2},{2,0},{1,3},{3,1},{4,6},{6,4},{5,7},{7,5},{8,10},{10,8},{9,1... | collective-permute-start | bytes 3932168 | tf_op jit(solution)/shard_map/ppermute | solution.py:435
  17.7 20.7 %collective-permute-start.5 = (bf16[4,64,1280]{2,1,0:T(8,128)(2,1)}, bf16[4,64,1280]{2,1,0:T(8,128)(2,1)S(1)}, u32[]{:S(2)}, u32[]{:S(2)}) collective-permute-start(bf16[4,64,1280]{2,1,0:T(8,128)(2,1)} %get-tuple-element.27), channel_id=1, source_target_pairs={{0,4},{4,1},{1,5},{5,0},{2,6},{6,3},{3,7},{7,2},{8,12},{12,9},{9,1... | collective-permute-start | bytes 1966088 | tf_op jit(solution)/shard_map/ppermute | solution.py:436
  19.2 21.3 %collective-permute-start.6 = (bf16[4,64,1280]{2,1,0:T(8,128)(2,1)}, bf16[4,64,1280]{2,1,0:T(8,128)(2,1)}, u32[]{:S(2)}, u32[]{:S(2)}) collective-permute-start(bf16[4,64,1280]{2,1,0:T(8,128)(2,1)} %get-tuple-element.28), channel_id=1, source_target_pairs={{0,5},{4,0},{1,4},{5,1},{2,7},{6,2},{3,6},{7,3},{8,13},{12,8},{9,1... | collective-permute-start | bytes 1966088 | tf_op jit(solution)/shard_map/ppermute | solution.py:437
  29.5 11.7 %copy-start.10 = (s32[32]{0:T(128)S(1)}, s32[32]{0:T(128)}, u32[]{:S(2)}) copy-start(s32[32]{0:T(128)} %prefix.1) | copy-start | bytes 388
  33.7 0.8 copy-start
  34.6 16.4 %collective-permute-start = (bf16[1280,256]{1,0:T(8,128)(2,1)}, bf16[1280,256]{1,0:T(8,128)(2,1)S(1)}, u32[]{:S(2)}, u32[]{:S(2)}) collective-permute-start(bf16[1280,256]{1,0:T(8,128)(2,1)} %after.1.refs_0_), channel_id=1, source_target_pairs={{0,64},{64,128},{128,192},{192,0},{1,65},{65,129},{129,193},{193,1... | collective-permute-start | bytes 1966088 | tf_op jit(solution)/shard_map/ppermute | solution.py:453
  35.9 15.1 %collective-permute-start.1 = (bf16[1280,256]{1,0:T(8,128)(2,1)}, bf16[1280,256]{1,0:T(8,128)(2,1)S(1)}, u32[]{:S(2)}, u32[]{:S(2)}) collective-permute-start(bf16[1280,256]{1,0:T(8,128)(2,1)} %after.1.refs_0_), channel_id=1, source_target_pairs={{0,192},{64,0},{128,64},{192,128},{1,193},{65,1},{129,65},{193,129... | collective-permute-start | bytes 1966088 | tf_op jit(solution)/shard_map/ppermute | solution.py:454
  38.3 15.9 %collective-permute-start.7 = (bf16[4,64,1280]{2,1,0:T(8,128)(2,1)S(1)}, bf16[4,64,1280]{2,1,0:T(8,128)(2,1)}, u32[]{:S(2)}, u32[]{:S(2)}) collective-permute-start(bf16[4,64,1280]{2,1,0:T(8,128)(2,1)S(1)} %collective-permute-done.5.refs_5_.refs_4_), channel_id=1, source_target_pairs={{0,2},{2,0},{1,3},{3,1},{4,6},{6,4},{5,7},{7,5},{8,10},{10,8},{9,1... | collective-permute-start | bytes 1966088 | tf_op jit(solution)/shard_map/ppermute | solution.py:438
  40.4 13.8 %collective-permute-start.8 = (bf16[4,64,1280]{2,1,0:T(8,128)(2,1)}, bf16[4,64,1280]{2,1,0:T(8,128)(2,1)}, u32[]{:S(2)}, u32[]{:S(2)}) collective-permute-start(bf16[4,64,1280]{2,1,0:T(8,128)(2,1)} %collective-permute-done.6.refs_6_.refs_5_), channel_id=1, source_target_pairs={{0,2},{2,0},{1,3},{3,1},{4,6},{6,4},{5,7},{7,5},{8,10},{10,8},{9,1... | collective-permute-start | bytes 1966088 | tf_op jit(solution)/shard_map/ppermute | solution.py:438
  41.5 1.1 copy-start.1
  42.5 11.7 %copy-start.2 = (bf16[1280,256]{1,0:T(8,128)(2,1)S(1)}, bf16[1280,256]{1,0:T(8,128)(2,1)}, u32[]{:S(2)}) copy-start(bf16[1280,256]{1,0:T(8,128)(2,1)} %after.1.refs_0_) | copy-start | bytes 1966084
  51.0 8.3 %collective-permute-start.3 = (bf16[640,256]{1,0:T(8,128)(2,1)S(1)}, bf16[640,256]{1,0:T(8,128)(2,1)S(1)}, u32[]{:S(2)}, u32[]{:S(2)}) collective-permute-start(bf16[640,256]{1,0:T(8,128)(2,1)S(1)} %get-tuple-element.25), channel_id=1, source_target_pairs={{0,64},{64,128},{128,192},{192,0},{1,65},{65,129},{129,193},{193,1... | collective-permute-start | bytes 983048 | tf_op jit(solution)/shard_map/ppermute | solution.py:457
  52.1 7.2 %collective-permute-start.4 = (bf16[640,256]{1,0:T(8,128)(2,1)S(1)}, bf16[640,256]{1,0:T(8,128)(2,1)S(1)}, u32[]{:S(2)}, u32[]{:S(2)}) collective-permute-start(bf16[640,256]{1,0:T(8,128)(2,1)S(1)} %get-tuple-element.26), channel_id=1, source_target_pairs={{0,192},{64,0},{128,64},{192,128},{1,193},{65,1},{129,65},{193,129... | collective-permute-start | bytes 983048 | tf_op jit(solution)/shard_map/ppermute | solution.py:457
  58.0 10.1 %copy-start.8 = (s32[32]{0:T(128)S(1)}, s32[32]{0:T(128)}, u32[]{:S(2)}) copy-start(s32[32]{0:T(128)} %dest.1) | copy-start | bytes 388
  58.0 14.0 %copy-start.7 = (bf16[32,128,128]{2,1,0:T(8,128)(2,1)S(1)}, bf16[32,128,128]{2,1,0:T(8,128)(2,1)}, u32[]{:S(2)}) copy-start(bf16[32,128,128]{2,1,0:T(8,128)(2,1)} %get-tuple-element.29.qp_ref) | copy-start | bytes 3145732
  58.0 14.0 %copy-start.9 = (s32[32]{0:T(128)S(1)}, s32[32]{0:T(128)}, u32[]{:S(2)}) copy-start(s32[32]{0:T(128)} %lengths.1) | copy-start | bytes 388
  59.3 12.7 %copy-start.3 = (f32[32,128,128]{2,1,0:T(8,128)S(1)}, f32[32,128,128]{2,1,0:T(8,128)}, u32[]{:S(2)}) copy-start(f32[32,128,128]{2,1,0:T(8,128)} %get-tuple-element.24.refs_1_.lse_ref) | copy-start | bytes 6291460
  59.3 12.7 %copy-start.5 = (f32[32,128,128]{2,1,0:T(8,128)S(1)}, f32[32,128,128]{2,1,0:T(8,128)}, u32[]{:S(2)}) copy-start(f32[32,128,128]{2,1,0:T(8,128)} %get-tuple-element.30.old_ref) | copy-start | bytes 6291460
  62.2 6.1 %collective-permute-start.10 = (bf16[128,384]{1,0:T(8,128)(2,1)S(1)}, bf16[128,384]{1,0:T(8,128)(2,1)S(1)}, u32[]{:S(2)}, u32[]{:S(2)}) collective-permute-start(bf16[128,384]{1,0:T(8,128)(2,1)S(1)} %get-tuple-element.34), channel_id=1, source_target_pairs={{0,4},{2,6},{4,0},{6,2},{1,5},{3,7},{5,1},{7,3},{8,12},{10,14},{12... | collective-permute-start | bytes 294920 | tf_op jit(solution)/shard_map/ppermute | solution.py:461
  65.2 6.7 %collective-permute-start.11 = (bf16[128,384]{1,0:T(8,128)(2,1)S(1)}, bf16[128,384]{1,0:T(8,128)(2,1)S(1)}, u32[]{:S(2)}, u32[]{:S(2)}) collective-permute-start(bf16[128,384]{1,0:T(8,128)(2,1)S(1)} %get-tuple-element.33), channel_id=1, source_target_pairs={{0,6},{2,4},{4,2},{6,0},{1,7},{3,5},{5,3},{7,1},{8,14},{10,12},{12... | collective-permute-start | bytes 294920 | tf_op jit(solution)/shard_map/ppermute | solution.py:461
  67.8 4.2 %collective-permute-start.9 = (bf16[128,384]{1,0:T(8,128)(2,1)S(1)}, bf16[128,384]{1,0:T(8,128)(2,1)S(1)}, u32[]{:S(2)}, u32[]{:S(2)}) collective-permute-start(bf16[128,384]{1,0:T(8,128)(2,1)S(1)} %get-tuple-element.35), channel_id=1, source_target_pairs={{0,2},{2,0},{4,6},{6,4},{1,3},{3,1},{5,7},{7,5},{8,10},{10,8},{12,... | collective-permute-start | bytes 294920 | tf_op jit(solution)/shard_map/ppermute | solution.py:461
  78.2 56.2 %all-to-all-start.1 = ((bf16[32,2,128,128]{3,2,1,0:T(8,128)(2,1)}), bf16[32,2,128,128]{3,2,1,0:T(8,128)(2,1)S(1)}, u32[]{:S(2)}, u32[]{:S(2)}) async-start(bf16[32,2,128,128]{3,2,1,0:T(8,128)(2,1)} %get-tuple-element.32), calls=%async_computation.1 | async-start | bytes 4194304 | tf_op jit(solution)/shard_map/all_to_all | solution.py:467

commit v3 on v2

--- a/solution.py
+++ b/solution.py
@@ -231,14 +231,15 @@
 
 def project_kernel(shifts, sources, carried, last, me, *refs):
     weights, refs = refs[: len(shifts)], refs[len(shifts) :]
-    own, near, *far = refs[: 2 if sources == 2 else 6]
+    count = 2 if sources == 2 else 6
+    own, near, *far = refs[:count]
     out_ref = refs[-1]
     half = TOKENS // 2
     places = [(own, 0, 0, TOKENS), (near, 1, 0, TOKENS)]
     for n, ref in enumerate(far):
         places.append((ref, 2 + n // 2, n % 2 * half, n % 2 * half + half))
     for ref, j, start, stop in places:
-        total = refs[-2][j, start:stop] if j < carried else None
+        total = refs[count][j, start:stop] if j < carried else None
         at = 0
         for n, (shift, weight) in enumerate(zip(shifts, weights)):
             if n == 0 and j < carried and shift == 0:
@@ -258,7 +259,7 @@
             out_ref[j, start:stop] = total
 
 
-def project(me, shifts, weights, inputs, total, last):
+def project(me, shifts, weights, inputs, total, last, *later):
     width, dtype = (3 * HEAD, BF16) if last else (2 * HEAD, F32)
     sources = 2 if len(inputs) == 2 else N_GEN
     carried = () if total is None else (total,)
@@ -267,13 +268,14 @@
             project_kernel, shifts, sources, 0 if total is None else total.shape[0], last
         ),
         in_specs=[pl.BlockSpec(memory_space=pltpu.SMEM)]
-        + [whole()] * (len(weights) + len(inputs) + len(carried)),
+        + [whole()] * (len(weights) + len(inputs) + len(carried))
+        + [pl.BlockSpec(memory_space=pl.ANY)] * len(later),
         out_specs=whole(),
         out_shape=jax.ShapeDtypeStruct((sources, TOKENS, width), dtype),
         compiler_params=params(),
         cost_estimate=SMALL,
         name="project",
-    )(me, *weights, *inputs, *carried)
+    )(me, *weights, *inputs, *carried, *later)
 
 
 FRESH_BLOCK = 16
@@ -282,11 +284,12 @@
 
 def fresh_kernel(
     dest, slot, lengths, me, p0, p1, p2, p3, cos_ref, sin_ref, qp_ref, lse_ref, old_ref,
-    kv_ref, out_ref,
+    q_one, lse_one, *refs,
 ):
-    step = pl.program_id(0)
-
-    @pl.when(step == 0)
+    kv_ref, out_ref, more_ref = refs[-3:]
+    step = ROLL // FRESH_BLOCK - 1 - pl.program_id(0)
+
+    @pl.when(pl.program_id(0) == 0)
     def _():
         cosine, sine = cos_ref[...], sin_ref[...]
         for j, part in enumerate((p0, p1, p2, p3)):
@@ -297,6 +300,8 @@
             kv_ref[0, g] = key.astype(BF16)
             kv_ref[1, g] = part[:, 2 * HEAD :]
         out_ref[...] = jnp.zeros_like(out_ref)
+        more_ref[...] = jnp.zeros_like(more_ref)
+        late_rows(me, dest, slot, lengths, q_one, lse_one, kv_ref, out_ref)
 
     wide = QUAD * STEPS * HEADS
     row, col = iota((QUAD * TOKENS, wide), 0), iota((QUAD * TOKENS, wide), 1)
@@ -340,7 +345,7 @@
     weight = [jnp.exp(s - t) for s, t in zip(score, top)]
     share = [jnp.exp(old - t) for old, t in zip(lse, top)]
     total = [jnp.sum(w, axis=1, keepdims=True) + a for w, a in zip(weight, share)]
-    for n in groups:
+    for n in reversed(groups):
         first = step * FRESH_BLOCK + n * QUAD
         length = lengths[first]
         for k in range(1, QUAD):
@@ -351,32 +356,187 @@
             (weight[n] * scale).astype(BF16), fresh[1][n], preferred_element_type=F32
         )
         mixed = mixed.astype(BF16)
-        for k in range(QUAD):
-            out_ref[dest[first + k], slot[first + k]] = mixed[k * TOKENS : (k + 1) * TOKENS]
+        for k in reversed(range(QUAD)):
+            d, j = dest[first + k], slot[first + k]
+            row = mixed[k * TOKENS : (k + 1) * TOKENS]
+            out_ref[d, :TOKENS] = row
+            more_ref[jnp.where(j == 1, d, N_FSDP)] = row
+
+
+def late_rows(me, dest, slot, lengths, q_one, lse_one, kv_ref, out_ref):
+    r = me[2]
+    start = pl.multiple_of(r // QUAD * 16, 16)
+    keys, values = (
+        jnp.concatenate([kv_ref[kind, g, pl.ds(start, 16)] for g in range(HEADS)], axis=0)
+        for kind in range(2)
+    )
+    score = lax.dot_general(
+        keys, q_one[0], (((1,), (1,)), ((), ())), preferred_element_type=F32
+    )
+    row, lane = iota((64, TOKENS), 0), iota((64, TOKENS), 1)
+    own = (
+        (row // 16 == lane // 32)
+        & (row % 16 // STEPS == r % QUAD)
+        & (row % STEPS <= lane % STEPS)
+    )
+    score = jnp.where(own, score * SCALE, masked_score)
+    eye = iota((TOKENS, TOKENS), 0) == iota((TOKENS, TOKENS), 1)
+    old = jnp.sum(jnp.where(eye, lse_one[0], 0.0), axis=0, keepdims=True)
+    top = jnp.maximum(jnp.max(score, axis=0, keepdims=True), old)
+    weight, share = jnp.exp(score - top), jnp.exp(old - top)
+    total = jnp.sum(weight, axis=0, keepdims=True) + share
+    kept = (iota((1, TOKENS), 1) % STEPS) < lengths[r]
+    scale = jnp.where(kept, 1.0 / total, 0.0)
+    weight, share = weight * scale, share * scale
+    rows = weight[0:8]
+    for n in range(8, 64, 8):
+        rows = rows + weight[n : n + 8]
+    rows = rows + pltpu.roll(rows, 4, 0)
+    place = iota((8, TOKENS), 0)
+    rows = jnp.where(place < 4, rows, jnp.where(place == 4, share, 0.0))
+    rows = jnp.concatenate([rows, jnp.zeros_like(rows)], axis=0)
+    pick = (
+        iota((16, 64), 1) == iota((16, 64), 0) // 4 * 16 + r % QUAD * 4 + iota((16, 64), 0) % 4
+    ).astype(BF16)
+    values = jnp.dot(pick, values, preferred_element_type=F32).astype(BF16)
+    seconds = lax.fori_loop(0, ROLL, lambda n, a: a + (slot[n] > 0).astype(jnp.int32), 0)
+    count = jnp.where(iota((16, TOKENS), 0) == 5, seconds.astype(F32), 0.0)
+    for d in range(N_FSDP):
+        out_ref[d, TOKENS + 16 :] = count.astype(BF16)
+    d = dest[r]
+    out_ref[d, TOKENS : TOKENS + 16] = values
+    out_ref[d, TOKENS + 16 :] = (rows + count).astype(BF16)
 
 
 def fresh(dest, slot, lengths, me, parts, cosine, sine, queries, lse, old):
     def whole_block(shape):
         return pl.BlockSpec(shape, lambda i, *_: (0,) * len(shape))
 
-    inside = pl.BlockSpec((FRESH_BLOCK, TOKENS, HEAD), lambda i, *_: (i, 0, 0))
+    steps = ROLL // FRESH_BLOCK
+    inside = pl.BlockSpec((FRESH_BLOCK, TOKENS, HEAD), lambda i, *_: (steps - 1 - i, 0, 0))
+    one = pl.BlockSpec((1, TOKENS, HEAD), lambda i, dest, slot, lengths, me: (me[2], 0, 0))
     kv = (2, HEADS, TOKENS, HEAD)
-    out = (N_FSDP, SLOTS, TOKENS, HEAD)
+    out = (N_FSDP, TOKENS + 32, HEAD)
+    more = (N_FSDP + 1, TOKENS, HEAD)
     return pl.pallas_call(
         fresh_kernel,
         grid_spec=pltpu.PrefetchScalarGridSpec(
             num_scalar_prefetch=4,
-            grid=(ROLL // FRESH_BLOCK,),
+            grid=(steps,),
             in_specs=[whole_block((TOKENS, 3 * HEAD))] * 4
             + [whole_block((TOKENS, HEAD))] * 2
-            + [inside] * 3,
-            out_specs=(whole_block(kv), whole_block(out)),
+            + [inside] * 3
+            + [one] * 2,
+            out_specs=(whole_block(kv), whole_block(out), whole_block(more)),
         ),
-        out_shape=(jax.ShapeDtypeStruct(kv, BF16), jax.ShapeDtypeStruct(out, BF16)),
+        out_shape=tuple(jax.ShapeDtypeStruct(shape, BF16) for shape in (kv, out, more)),
         compiler_params=params(),
         cost_estimate=SMALL,
         name="fresh",
-    )(dest, slot, lengths, me, *parts, cosine, sine, queries, lse, old)
+    )(dest, slot, lengths, me, *parts, cosine, sine, queries, lse, old, queries, lse)
+
+
+def second_kernel(me, old_ref, _, out_ref):
+    row = old_ref[0].astype(BF16)
+    for z in range(N_Z):
+        out_ref[z] = row
+
+
+def second(me, old, later):
+    return pl.pallas_call(
+        second_kernel,
+        grid_spec=pltpu.PrefetchScalarGridSpec(
+            num_scalar_prefetch=1,
+            grid=(1,),
+            in_specs=[
+                pl.BlockSpec((1, TOKENS, HEAD), lambda i, me: (me[2], 0, 0)),
+                pl.BlockSpec(memory_space=pl.ANY),
+            ],
+            out_specs=pl.BlockSpec((N_Z, TOKENS, HEAD), lambda i, me: (0, 0, 0)),
+        ),
+        out_shape=jax.ShapeDtypeStruct((N_Z, TOKENS, HEAD), BF16),
+        compiler_params=params(),
+        cost_estimate=SMALL,
+        name="second",
+    )(me, old, later)
+
+
+def join_kernel(me, in_ref, e0, e1, e2, e3, _, out_ref, most_ref, seen_ref):
+    step = pl.program_id(0)
+
+    @pl.when(step == 0)
+    def _():
+        seen_ref[...] = jnp.zeros_like(seen_ref)
+
+    eye = iota((TOKENS, TOKENS), 0) == iota((TOKENS, TOKENS), 1)
+    row8 = iota((8, 128), 0)
+    same = iota((16, 128), 1) // 32 == iota((16, 128), 0) // 4
+    block = range(N_Z)
+
+    def body(extra):
+        for n in block:
+            out_ref[n, 0] = in_ref[n, :TOKENS]
+        tiles = [in_ref[n, TOKENS + 16 :, :].astype(F32)[:8] for n in block]
+        most = tiles[0]
+        for tile in tiles[1:]:
+            most = jnp.maximum(most, tile)
+        seen_ref[...] = jnp.maximum(seen_ref[...], most)
+        diags = [jnp.where(eye, tile[4:5], 0.0).astype(BF16) for tile in tiles]
+        both = [jnp.where(row8 < 4, tile, pltpu.roll(tile, 4, 0)) for tile in tiles]
+        weights = [
+            jnp.where(same, jnp.concatenate([w, w], axis=0), 0.0).astype(BF16) for w in both
+        ]
+        kept = [
+            jnp.dot(diags[n], extra[n], preferred_element_type=F32) for n in block
+        ]
+        added = [
+            lax.dot_general(
+                weights[n],
+                in_ref[n, TOKENS : TOKENS + 16, :],
+                (((0,), (0,)), ((), ())),
+                preferred_element_type=F32,
+            )
+            for n in block
+        ]
+        for n in block:
+            out_ref[n, 1] = (kept[n] + added[n]).astype(BF16)
+
+    for k, extra in enumerate((e0, e1, e2, e3)):
+        pl.when(step == k)(functools.partial(body, extra))
+
+    @pl.when(step == pl.num_programs(0) - 1)
+    def _():
+        most_ref[0] = jnp.max(seen_ref[5:6, :]).astype(jnp.int32)
+
+
+def join(me, rows, extras, later):
+    def of_source(i, me):
+        return (me[0] + N_Y - i) % N_Y
+
+    return pl.pallas_call(
+        join_kernel,
+        grid_spec=pltpu.PrefetchScalarGridSpec(
+            num_scalar_prefetch=1,
+            grid=(N_Y,),
+            in_specs=[pl.BlockSpec((N_Z, TOKENS + 32, HEAD), lambda i, me: (of_source(i, me), 0, 0))]
+            + [pl.BlockSpec((N_Z, TOKENS, HEAD), lambda i, me: (0, 0, 0))] * 4
+            + [pl.BlockSpec(memory_space=pl.ANY)],
+            out_specs=(
+                pl.BlockSpec(
+                    (N_Z, SLOTS, TOKENS, HEAD), lambda i, me: (of_source(i, me), 0, 0, 0)
+                ),
+                pl.BlockSpec(memory_space=pltpu.SMEM),
+            ),
+            scratch_shapes=[pltpu.VMEM((8, HEAD), F32)],
+        ),
+        out_shape=(
+            jax.ShapeDtypeStruct((N_FSDP, SLOTS, TOKENS, HEAD), BF16),
+            jax.ShapeDtypeStruct((1,), jnp.int32),
+        ),
+        compiler_params=params(),
+        cost_estimate=SMALL,
+        name="join",
+    )(me, rows, *extras, later)
 
 
 def in_rows(joined):
@@ -449,24 +609,33 @@
         own,
     )
     own_rows = after(own_rows, lse)
-    me = jnp.stack([lax.axis_index("y"), lax.axis_index("xl") * 2 + lax.axis_index("c")])
+    one = jnp.argmax(slot_rank).astype(jnp.int32)
+    me = jnp.stack([lax.axis_index("y"), lax.axis_index("xl") * 2 + lax.axis_index("c"), one])
     before = lax.ppermute(own_rows, "y", shift_y(1))
     beyond = lax.ppermute(own_rows, "y", shift_y(-1))
     total = project(me, (0,), (own_rows,), inputs[:2], None, False)
+    extra = lax.all_to_all(second(me, old_rows, total), "z", 0, 0, tiled=True)
     low, high = halves(before, beyond, total)
     across = [lax.ppermute(low, "y", shift_y(1)), lax.ppermute(high, "y", shift_y(-1))]
     total = project(me, (0, 1, 3), (own_rows, before, beyond), inputs, total, False)
-    parts = project(me, (2, 2), across, inputs, total, True)
+    parts = project(me, (2, 2), across, inputs, total, True, extra)
     parts = [parts[0]] + [
         lax.ppermute(parts[j], ("xl", "c"), [(q, q ^ j) for q in range(N_GEN)]) for j in (1, 2, 3)
     ]
     cosine, sine = turn_tables(prefix_lengths)
-    fresh_parts, rows = fresh(
+    fresh_parts, rows, more = fresh(
         destinations, slot_rank, rollout_lengths, me, parts, cosine, sine, ordered, lse, old_rows
     )
     rows = lax.all_to_all(rows, ("y", "z"), 0, 0, tiled=True)
+    extras = [extra] + [lax.ppermute(extra, "y", shift_y(k)) for k in (1, 2, 3)]
     fresh_kv = fresh_parts.reshape(2, HEADS, ROLL, STEPS, HEAD).transpose(2, 3, 0, 1, 4)
-    returned_rows = in_rows(rows)
+    joined, most = join(me, rows, extras, fresh_kv)
+
+    def with_all_seconds():
+        seconds = lax.all_to_all(more[:N_FSDP], ("y", "z"), 0, 0, tiled=True)
+        return jnp.stack([joined[:, 0], seconds], axis=1)
+
+    returned_rows = in_rows(after(lax.cond(most[0] > 1, with_all_seconds, lambda: joined)))
     return (new_master, new_first, new_second, fresh_kv, returned_rows)
 
 

time: 136 us -> 131 us (0.963)
  waiting for transfers between devices: 67.1 us -> 38.8 us
  starting transfers between devices: 33.4 us -> 45.4 us
  Pallas kernels: 28.2 us -> 35.4 us
  other arithmetic: 0.74 us -> 2.16 us
    all_to_all x1, waiting for transfers between devices: 48.8 us -> 8.43 us  [on_device(): rows = lax.all_to_all(rows, ('y', 'z'), 0, 0, tiled=True)]
    ppermute x0 -> x3, waiting for transfers between devices: none -> 19.9 us  [on_device(): extras = [extra] + [lax.ppermute(extra, 'y', shift_y(k)) for k in (1, 2, 3)]]
    ppermute x1, waiting for transfers between devices: 6.71 us -> 0.01 us  [on_device(): before = lax.ppermute(own_rows, 'y', shift_y(1))]
    all_to_all x0 -> x1, starting transfers between devices: none -> 5.31 us  [on_device(): extra = lax.all_to_all(second(me, old_rows, total), 'z', 0, 0, tiled=True)]
    ppermute x0 -> x3, starting transfers between devices: none -> 4.89 us  [on_device(): extras = [extra] + [lax.ppermute(extra, 'y', shift_y(k)) for k in (1, 2, 3)]]
    pallas_call x0 -> x2, Pallas kernels: none -> 4.56 us  [the longest x1 3.3 us: join(): pl.pallas_call(join_kernel, grid_spec=pltpu.PrefetchScalarGridSpec(num_sc...]
    all_to_all x1, starting transfers between devices: 6.39 us -> 9.27 us  [on_device(): rows = lax.all_to_all(rows, ('y', 'z'), 0, 0, tiled=True)]
    pallas_call x1, Pallas kernels: 0.04 us -> 2.14 us  [halves(): pl.pallas_call(halves_kernel, in_specs=[whole(), whole(), pl.BlockSpec(me...]
  transfers between devices with their start and end apart: 14 -> 18, of which waited for: 7 -> 7; matrix products, arithmetic and copies ran while one was open for 1% -> 2% of each run, Pallas kernels for 12% -> 16%
where the time goes in v3:
time: 131 us; the launch traced here: 130 us
  starting transfers between devices  45.4 us (35%)
  waiting for transfers between devices  38.8 us (30%)
  Pallas kernels  35.4 us (27%)
  local copies, waits for them, and re-layouts  6.51 us (5%)
  other arithmetic  2.16 us (2%)
  between operations  1.68 us (1%)
    ppermute x3, waiting for transfers between devices, on_device(): extras = [extra] + [lax.ppermute(extra, 'y', shift_y(k)) for k in (1, 2, 3)]  19.9 us
    all_to_all x1, starting transfers between devices, on_device(): lax.all_to_all(blocks.reshape(N_Z * N_GEN, ROWS, 2 * HEAD), ('z', 'xl', '...  11.1 us
    all_to_all x1, starting transfers between devices, on_device(): rows = lax.all_to_all(rows, ('y', 'z'), 0, 0, tiled=True)  9.27 us
    pallas_call x1, Pallas kernels, old_attention(): pl.pallas_call(old_kernel, grid_spec=pltpu.PrefetchScalarGridSpec(num_sca...  9.03 us
    pallas_call x3, Pallas kernels, project(): pl.pallas_call(functools.partial(project_kernel, shifts, sources, 0 if to...  8.93 us
    all_to_all x1, waiting for transfers between devices, on_device(): rows = lax.all_to_all(rows, ('y', 'z'), 0, 0, tiled=True)  8.43 us
    pallas_call x1, Pallas kernels, fresh(): pl.pallas_call(fresh_kernel, grid_spec=pltpu.PrefetchScalarGridSpec(num_s...  6.32 us
    unnamed x32, local copies, waits for them, and re-layouts  6.16 us
  transfers between devices with their start and end apart: 18, of which 7 were waited for; matrix products, arithmetic and copies ran while one was open for 2% of the time, Pallas kernels for 16%

profile of v3, /device:TPU:1, one launch (start us, length us, event | category | flops | bytes accessed | tf_op | source)
XLA Modules:
  0.0 129.9 jit_solution(10245421764244837174)
XLA Ops:
  0.6 2.4 %adam.1 = (f32[2,40,512]{2,1,0:T(8,128)}, f32[2,40,512]{2,1,0:T(8,128)}, f32[2,40,512]{2,1,0:T(8,128)}, bf16[8,4,40,256]{3,2,1,0:T(8,128)(2,1)}) custom-call(f32[2,40,512]{2,1,0:T(8,128)} %refs_0_.1, f32[2,40,512]{2,1,0:T(8,128)} %refs_1_.1, f32[2,40,512]{2,1,0:T(8,128)} %refs_2_.1, f32[2,40,512]{2,1,0:T(8,128)} %refs_3_.1), custom_call_target="tpu_custom_call" | custom-call | flops 1000 | bytes 1000 | tf_op jit(solution)/shard_map/adam/pallas_call | solution.py:98
  3.1 11.1 %all-to-all-start.1 = ((bf16[32,40,256]{2,1,0:T(8,128)(2,1)}), bf16[32,40,256]{2,1,0:T(8,128)(2,1)S(1)}, u32[]{:S(2)}, u32[]{:S(2)}) async-start(bf16[32,40,256]{2,1,0:T(8,128)(2,1)} %bitcast.27), calls=%async_computation.1 | async-start | bytes 1310720 | tf_op jit(solution)/shard_map/all_to_all | solution.py:587
  14.1 1.1 copy-done.7
  15.3 2.0 %columns.1 = (bf16[4,128,1280]{2,1,0:T(8,128)(2,1)}, bf16[4,64,1280]{2,1,0:T(8,128)(2,1)}, bf16[4,64,1280]{2,1,0:T(8,128)(2,1)S(1)}) custom-call(bf16[32,4,5120]{2,1,0:T(4,128)(2,1)S(1)} %copy-done.11, bf16[8,4,40,256]{3,2,1,0:T(8,128)(2,1)S(1)} %copy-done.7), custom_call_target="tpu_custom_call" | custom-call | flops 1000 | bytes 1000 | tf_op jit(solution)/shard_map/columns/pallas_call | solution.py:127
  17.5 1.5 %collective-permute-start.5 = (bf16[4,64,1280]{2,1,0:T(8,128)(2,1)}, bf16[4,64,1280]{2,1,0:T(8,128)(2,1)S(1)}, u32[]{:S(2)}, u32[]{:S(2)}) collective-permute-start(bf16[4,64,1280]{2,1,0:T(8,128)(2,1)} %get-tuple-element.42), channel_id=1, source_target_pairs={{0,4},{4,1},{1,5},{5,0},{2,6},{6,3},{3,7},{7,2},{8,12},{12,9},{9,1... | collective-permute-start | bytes 1966088 | tf_op jit(solution)/shard_map/ppermute | solution.py:596
  19.0 1.3 collective-permute-start.6
  20.2 9.0 %old_attention.1 = (f32[32,128,128]{2,1,0:T(8,128)}, f32[32,128,128]{2,1,0:T(8,128)}, bf16[32,128,128]{2,1,0:T(8,128)(2,1)}) custom-call(s32[32]{0:T(128)} %prefix.1, bf16[32,128,128]{2,1,0:T(8,128)(2,1)} %bitcast.34, bf16[32,512,128]{2,1,0:T(8,128)(2,1)} %bitcast.31, bf16[32,512,128]{2,1,0:T(8,128)(2,1)} %bitcast.32, ...), custom_call_target="tpu_custom_call" | custom-call | flops 1000 | bytes 1000 | tf_op jit(solution)/shard_map/old_attention/pallas_call | solution.py:193
  29.3 4.5 %all-to-all-done.1 = bf16[32,40,256]{2,1,0:T(8,128)(2,1)S(1)} async-done(((bf16[32,40,256]{2,1,0:T(8,128)(2,1)}), bf16[32,40,256]{2,1,0:T(8,128)(2,1)S(1)}, u32[]{:S(2)}, u32[]{:S(2)}) %all-to-all-start.1) | async-done | bytes 655392 | tf_op jit(solution)/shard_map/all_to_all | solution.py:587
  34.6 1.3 collective-permute-start
  35.9 1.4 %collective-permute-start.1 = (bf16[1280,256]{1,0:T(8,128)(2,1)}, bf16[1280,256]{1,0:T(8,128)(2,1)}, u32[]{:S(2)}, u32[]{:S(2)}) collective-permute-start(bf16[1280,256]{1,0:T(8,128)(2,1)} %after.2.refs_0_), channel_id=1, source_target_pairs={{0,192},{64,0},{128,64},{192,128},{1,193},{65,1},{129,65},{193,129... | collective-permute-start | bytes 1966088 | tf_op jit(solution)/shard_map/ppermute | solution.py:615
  38.3 1.8 %collective-permute-start.7 = (bf16[4,64,1280]{2,1,0:T(8,128)(2,1)S(1)}, bf16[4,64,1280]{2,1,0:T(8,128)(2,1)}, u32[]{:S(2)}, u32[]{:S(2)}) collective-permute-start(bf16[4,64,1280]{2,1,0:T(8,128)(2,1)S(1)} %collective-permute-done.5.refs_5_.refs_4_), channel_id=1, source_target_pairs={{0,2},{2,0},{1,3},{3,1},{4,6},{6,4},{5,7},{7,5},{8,10},{10,8},{9,1... | collective-permute-start | bytes 1966088 | tf_op jit(solution)/shard_map/ppermute | solution.py:598
  41.9 1.1 copy-done.2
  43.0 1.8 %project.3._.refs_9_ = f32[2,128,256]{2,1,0:T(8,128)S(1)} custom-call(s32[3]{0:T(128)S(1)} %pad_add_fusion.me, bf16[1280,256]{1,0:T(8,128)(2,1)S(1)} %copy-done.2, bf16[4,128,1280]{2,1,0:T(8,128)(2,1)} %get-tuple-element.38._.refs_1_.refs_3_.refs_2_, bf16[4,128,1280]{2,1,0:T(8,128)(2,1)S(1)} %collective-permute-done.2.refs_2_.refs_4_.refs_3_), custom_call_target="tpu_custom_call" | custom-call | flops 1000 | bytes 1000 | tf_op jit(solution)/shard_map/project/pallas_call | solution.py:266
  44.9 1.3 second.1
  46.2 5.3 %all-to-all-start.2 = ((bf16[8,128,128]{2,1,0:T(8,128)(2,1)}), bf16[8,128,128]{2,1,0:T(8,128)(2,1)S(1)}, u32[]{:S(2)}, u32[]{:S(2)}) async-start(bf16[8,128,128]{2,1,0:T(8,128)(2,1)} %second.1), calls=%async_computation.2 | async-start | bytes 524288 | tf_op jit(solution)/shard_map/all_to_all | solution.py:617
  51.7 2.1 %halves.1 = (bf16[640,256]{1,0:T(8,128)(2,1)}, bf16[640,256]{1,0:T(8,128)(2,1)}) custom-call(bf16[1280,256]{1,0:T(8,128)(2,1)} %collective-permute-done.before.refs_1_, bf16[1280,256]{1,0:T(8,128)(2,1)} %collective-permute-done.1.beyond.refs_2_, f32[2,128,256]{2,1,0:T(8,128)S(1)} %project.3._.refs_9_), custom_call_target="tpu_custom_call" | custom-call | flops 1000 | bytes 1000 | tf_op jit(solution)/shard_map/halves/pallas_call | solution.py:221
  53.9 1.3 collective-permute-start.3
  55.2 1.4 %collective-permute-start.4 = (bf16[640,256]{1,0:T(8,128)(2,1)}, bf16[640,256]{1,0:T(8,128)(2,1)}, u32[]{:S(2)}, u32[]{:S(2)}) collective-permute-start(bf16[640,256]{1,0:T(8,128)(2,1)} %get-tuple-element.41), channel_id=1, source_target_pairs={{0,192},{64,0},{128,64},{192,128},{1,193},{65,1},{129,65},{193,129... | collective-permute-start | bytes 983048 | tf_op jit(solution)/shard_map/ppermute | solution.py:619
  57.0 4.1 %project.4.refs_8_ = f32[4,128,256]{2,1,0:T(8,128)S(1)} custom-call(s32[3]{0:T(128)S(1)} %pad_add_fusion.me, bf16[1280,256]{1,0:T(8,128)(2,1)S(1)} %copy-done.3, bf16[1280,256]{1,0:T(8,128)(2,1)} %collective-permute-done.before.refs_1_, bf16[1280,256]{1,0:T(8,128)(2,1)} %collective-permute-done.1.beyond.refs_2_, ...), custom_call_target="tpu_custom_call" | custom-call | flops 1000 | bytes 1000 | tf_op jit(solution)/shard_map/project/pallas_call | solution.py:266
  61.9 2.0 %all-to-all-done.2.refs_9_.e0 = bf16[8,128,128]{2,1,0:T(8,128)(2,1)S(1)} async-done(((bf16[8,128,128]{2,1,0:T(8,128)(2,1)}), bf16[8,128,128]{2,1,0:T(8,128)(2,1)S(1)}, u32[]{:S(2)}, u32[]{:S(2)}) %all-to-all-start.2) | async-done | bytes 262176 | tf_op jit(solution)/shard_map/all_to_all | solution.py:617
  64.9 3.0 %project.5 = bf16[4,128,384]{2,1,0:T(8,128)(2,1)S(1)} custom-call(s32[3]{0:T(128)S(1)} %pad_add_fusion.me, bf16[640,256]{1,0:T(8,128)(2,1)} %collective-permute-done.3.refs_0_, bf16[640,256]{1,0:T(8,128)(2,1)} %collective-permute-done.4.refs_1_, bf16[4,128,1280]{2,1,0:T(8,128)(2,1)} %get-tuple-element.38._.refs_1_.refs_3_.refs_2_, ...), custom_call_target="tpu_custom_call" | custom-call | flops 1000 | bytes 1000 | tf_op jit(solution)/shard_map/project/pallas_call | solution.py:266
  69.0 2.8 %collective-permute-start.11 = (bf16[128,384]{1,0:T(8,128)(2,1)S(1)}, bf16[128,384]{1,0:T(8,128)(2,1)S(1)}, u32[]{:S(2)}, u32[]{:S(2)}) collective-permute-start(bf16[128,384]{1,0:T(8,128)(2,1)S(1)} %get-tuple-element.51), channel_id=1, source_target_pairs={{0,6},{2,4},{4,2},{6,0},{1,7},{3,5},{5,3},{7,1},{8,14},{10,12},{12... | collective-permute-start | bytes 294920 | tf_op jit(solution)/shard_map/ppermute | solution.py:623
  72.0 3.7 %collective-permute-done.11.p3 = bf16[128,384]{1,0:T(8,128)(2,1)S(1)} collective-permute-done((bf16[128,384]{1,0:T(8,128)(2,1)S(1)}, bf16[128,384]{1,0:T(8,128)(2,1)S(1)}, u32[]{:S(2)}, u32[]{:S(2)}) %collective-permute-start.11) | collective-permute-done | bytes 98336 | tf_op jit(solution)/shard_map/ppermute | solution.py:623
  75.7 6.3 %fresh.1 = (bf16[2,4,128,128]{3,2,1,0:T(8,128)(2,1)S(1)}, bf16[32,160,128]{2,1,0:T(8,128)(2,1)S(1)}, bf16[33,128,128]{2,1,0:T(8,128)(2,1)}) custom-call(s32[32]{0:T(128)S(1)} %copy-done.13, s32[32]{0:T(128)S(1)} %convert_reduce_fusion.slot, s32[32]{0:T(128)S(1)} %copy-done.14, s32[3]{0:T(128)S(1)} %pad_add_fusion.me, ...), custom_call_target="tpu_custom_call" | custom-call | flops 1000 | bytes 1000 | tf_op jit(solution)/shard_map/fresh/pallas_call | solution.py:421
  83.1 9.3 %all-to-all-start.3 = ((bf16[32,160,128]{2,1,0:T(8,128)(2,1)}), bf16[32,160,128]{2,1,0:T(8,128)(2,1)S(1)}, u32[]{:S(2)}, u32[]{:S(2)}) async-start(bf16[32,160,128]{2,1,0:T(8,128)(2,1)} %copy-done.10), calls=%async_computation.3 | async-start | bytes 2621440 | tf_op jit(solution)/shard_map/all_to_all | solution.py:629
  92.4 1.3 %collective-permute-start.12 = (bf16[8,128,128]{2,1,0:T(8,128)(2,1)S(1)}, bf16[8,128,128]{2,1,0:T(8,128)(2,1)S(1)}, u32[]{:S(2)}, u32[]{:S(2)}) collective-permute-start(bf16[8,128,128]{2,1,0:T(8,128)(2,1)S(1)} %all-to-all-done.2.refs_9_.e0), channel_id=1, source_target_pairs={{0,64},{64,128},{128,192},{192,0},{1,65},{65,129},{129,193},{193,1... | collective-permute-start | bytes 786440 | tf_op jit(solution)/shard_map/ppermute | solution.py:630
  93.7 2.4 %collective-permute-start.13 = (bf16[8,128,128]{2,1,0:T(8,128)(2,1)S(1)}, bf16[8,128,128]{2,1,0:T(8,128)(2,1)S(1)}, u32[]{:S(2)}, u32[]{:S(2)}) collective-permute-start(bf16[8,128,128]{2,1,0:T(8,128)(2,1)S(1)} %all-to-all-done.2.refs_9_.e0), channel_id=1, source_target_pairs={{0,128},{64,192},{128,0},{192,64},{1,129},{65,193},{129,1},{193,65... | collective-permute-start | bytes 786440 | tf_op jit(solution)/shard_map/ppermute | solution.py:630
  96.1 1.1 collective-permute-start.14
  97.5 9.6 %collective-permute-done.12.e1 = bf16[8,128,128]{2,1,0:T(8,128)(2,1)S(1)} collective-permute-done((bf16[8,128,128]{2,1,0:T(8,128)(2,1)S(1)}, bf16[8,128,128]{2,1,0:T(8,128)(2,1)S(1)}, u32[]{:S(2)}, u32[]{:S(2)}) %collective-permute-start.12) | collective-permute-done | bytes 262176 | tf_op jit(solution)/shard_map/ppermute | solution.py:630
  107.1 10.2 %collective-permute-done.13.e2 = bf16[8,128,128]{2,1,0:T(8,128)(2,1)S(1)} collective-permute-done((bf16[8,128,128]{2,1,0:T(8,128)(2,1)S(1)}, bf16[8,128,128]{2,1,0:T(8,128)(2,1)S(1)}, u32[]{:S(2)}, u32[]{:S(2)}) %collective-permute-start.13) | collective-permute-done | bytes 262176 | tf_op jit(solution)/shard_map/ppermute | solution.py:630
  117.3 8.4 %all-to-all-done.3.in_ref = bf16[32,160,128]{2,1,0:T(8,128)(2,1)S(1)} async-done(((bf16[32,160,128]{2,1,0:T(8,128)(2,1)}), bf16[32,160,128]{2,1,0:T(8,128)(2,1)S(1)}, u32[]{:S(2)}, u32[]{:S(2)}) %all-to-all-start.3) | async-done | bytes 1310752 | tf_op jit(solution)/shard_map/all_to_all | solution.py:629
  125.8 3.3 %join.1 = (bf16[32,2,128,128]{3,2,1,0:T(8,128)(2,1)}, s32[1]{0:T(128)}) custom-call(s32[3]{0:T(128)S(1)} %pad_add_fusion.me, bf16[32,160,128]{2,1,0:T(8,128)(2,1)S(1)} %all-to-all-done.3.in_ref, bf16[8,128,128]{2,1,0:T(8,128)(2,1)S(1)} %all-to-all-done.2.refs_9_.e0, bf16[8,128,128]{2,1,0:T(8,128)(2,1)S(1)} %collective-permute-done.12.e1, ...), custom_call_target="tpu_custom_call" | custom-call | flops 1000 | bytes 1000 | tf_op jit(solution)/shard_map/join/pallas_call | solution.py:516
  (59 shorter events, 8.8 us)
Async XLA Ops:
  0.6 13.5 %copy-start.11 = (bf16[32,4,5120]{2,1,0:T(4,128)(2,1)S(1)}, bf16[32,4,5120]{2,1,0:T(4,128)(2,1)}, u32[]{:S(2)}) copy-start(bf16[32,4,5120]{2,1,0:T(4,128)(2,1)} %x_ref.1) | copy-start | bytes 3932164
  3.1 30.7 %all-to-all-start.1 = ((bf16[32,40,256]{2,1,0:T(8,128)(2,1)}), bf16[32,40,256]{2,1,0:T(8,128)(2,1)S(1)}, u32[]{:S(2)}, u32[]{:S(2)}) async-start(bf16[32,40,256]{2,1,0:T(8,128)(2,1)} %bitcast.27), calls=%async_computation.1 | async-start | bytes 1310720 | tf_op jit(solution)/shard_map/all_to_all | solution.py:587
  14.1 1.1 copy-start.7
  17.2 24.6 %collective-permute-start.2 = (bf16[4,128,1280]{2,1,0:T(8,128)(2,1)}, bf16[4,128,1280]{2,1,0:T(8,128)(2,1)S(1)}, u32[]{:S(2)}, u32[]{:S(2)}) collective-permute-start(bf16[4,128,1280]{2,1,0:T(8,128)(2,1)} %get-tuple-element.38._.refs_1_.refs_3_.refs_2_), channel_id=1, source_target_pairs={{0,2},{2,0},{1,3},{3,1},{4,6},{6,4},{5,7},{7,5},{8,10},{10,8},{9,1... | collective-permute-start | bytes 3932168 | tf_op jit(solution)/shard_map/ppermute | solution.py:595
  17.5 20.8 %collective-permute-start.5 = (bf16[4,64,1280]{2,1,0:T(8,128)(2,1)}, bf16[4,64,1280]{2,1,0:T(8,128)(2,1)S(1)}, u32[]{:S(2)}, u32[]{:S(2)}) collective-permute-start(bf16[4,64,1280]{2,1,0:T(8,128)(2,1)} %get-tuple-element.42), channel_id=1, source_target_pairs={{0,4},{4,1},{1,5},{5,0},{2,6},{6,3},{3,7},{7,2},{8,12},{12,9},{9,1... | collective-permute-start | bytes 1966088 | tf_op jit(solution)/shard_map/ppermute | solution.py:596
  19.0 21.5 %collective-permute-start.6 = (bf16[4,64,1280]{2,1,0:T(8,128)(2,1)S(1)}, bf16[4,64,1280]{2,1,0:T(8,128)(2,1)}, u32[]{:S(2)}, u32[]{:S(2)}) collective-permute-start(bf16[4,64,1280]{2,1,0:T(8,128)(2,1)S(1)} %get-tuple-element.43), channel_id=1, source_target_pairs={{0,5},{4,0},{1,4},{5,1},{2,7},{6,2},{3,6},{7,3},{8,13},{12,8},{9,1... | collective-permute-start | bytes 1966088 | tf_op jit(solution)/shard_map/ppermute | solution.py:597
  29.3 8.1 %copy-start.13 = (s32[32]{0:T(128)S(1)}, s32[32]{0:T(128)}, u32[]{:S(2)}) copy-start(s32[32]{0:T(128)} %dest.1) | copy-start | bytes 388
  34.6 17.1 %collective-permute-start = (bf16[1280,256]{1,0:T(8,128)(2,1)}, bf16[1280,256]{1,0:T(8,128)(2,1)}, u32[]{:S(2)}, u32[]{:S(2)}) collective-permute-start(bf16[1280,256]{1,0:T(8,128)(2,1)} %after.2.refs_0_), channel_id=1, source_target_pairs={{0,64},{64,128},{128,192},{192,0},{1,65},{65,129},{129,193},{193,1... | collective-permute-start | bytes 1966088 | tf_op jit(solution)/shard_map/ppermute | solution.py:614
  35.9 15.8 %collective-permute-start.1 = (bf16[1280,256]{1,0:T(8,128)(2,1)}, bf16[1280,256]{1,0:T(8,128)(2,1)}, u32[]{:S(2)}, u32[]{:S(2)}) collective-permute-start(bf16[1280,256]{1,0:T(8,128)(2,1)} %after.2.refs_0_), channel_id=1, source_target_pairs={{0,192},{64,0},{128,64},{192,128},{1,193},{65,1},{129,65},{193,129... | collective-permute-start | bytes 1966088 | tf_op jit(solution)/shard_map/ppermute | solution.py:615
  38.3 18.6 %collective-permute-start.7 = (bf16[4,64,1280]{2,1,0:T(8,128)(2,1)S(1)}, bf16[4,64,1280]{2,1,0:T(8,128)(2,1)}, u32[]{:S(2)}, u32[]{:S(2)}) collective-permute-start(bf16[4,64,1280]{2,1,0:T(8,128)(2,1)S(1)} %collective-permute-done.5.refs_5_.refs_4_), channel_id=1, source_target_pairs={{0,2},{2,0},{1,3},{3,1},{4,6},{6,4},{5,7},{7,5},{8,10},{10,8},{9,1... | collective-permute-start | bytes 1966088 | tf_op jit(solution)/shard_map/ppermute | solution.py:598
  40.4 16.5 %collective-permute-start.8 = (bf16[4,64,1280]{2,1,0:T(8,128)(2,1)}, bf16[4,64,1280]{2,1,0:T(8,128)(2,1)}, u32[]{:S(2)}, u32[]{:S(2)}) collective-permute-start(bf16[4,64,1280]{2,1,0:T(8,128)(2,1)} %collective-permute-done.6.refs_6_.refs_5_), channel_id=1, source_target_pairs={{0,2},{2,0},{1,3},{3,1},{4,6},{6,4},{5,7},{7,5},{8,10},{10,8},{9,1... | collective-permute-start | bytes 1966088 | tf_op jit(solution)/shard_map/ppermute | solution.py:598
  41.9 1.1 copy-start.2
  43.0 2.0 %copy-start.4 = (f32[32,128,128]{2,1,0:T(8,128)S(1)}, f32[32,128,128]{2,1,0:T(8,128)}, u32[]{:S(2)}) copy-start(f32[32,128,128]{2,1,0:T(8,128)} %get-tuple-element.44.old_ref) | copy-start | bytes 6291460
  44.8 6.7 %copy-start.16 = (s32[32]{0:T(128)S(1)}, s32[32]{0:T(128)}, u32[]{:S(2)}) copy-start(s32[32]{0:T(128)} %prefix.1) | copy-start | bytes 388
  44.9 12.0 %copy-start.3 = (bf16[1280,256]{1,0:T(8,128)(2,1)S(1)}, bf16[1280,256]{1,0:T(8,128)(2,1)}, u32[]{:S(2)}) copy-start(bf16[1280,256]{1,0:T(8,128)(2,1)} %after.2.refs_0_) | copy-start | bytes 1966084
  46.2 17.7 %all-to-all-start.2 = ((bf16[8,128,128]{2,1,0:T(8,128)(2,1)}), bf16[8,128,128]{2,1,0:T(8,128)(2,1)S(1)}, u32[]{:S(2)}, u32[]{:S(2)}) async-start(bf16[8,128,128]{2,1,0:T(8,128)(2,1)} %second.1), calls=%async_computation.2 | async-start | bytes 524288 | tf_op jit(solution)/shard_map/all_to_all | solution.py:617
  53.9 10.0 %collective-permute-start.3 = (bf16[640,256]{1,0:T(8,128)(2,1)}, bf16[640,256]{1,0:T(8,128)(2,1)}, u32[]{:S(2)}, u32[]{:S(2)}) collective-permute-start(bf16[640,256]{1,0:T(8,128)(2,1)} %get-tuple-element.40), channel_id=1, source_target_pairs={{0,64},{64,128},{128,192},{192,0},{1,65},{65,129},{129,193},{193,1... | collective-permute-start | bytes 983048 | tf_op jit(solution)/shard_map/ppermute | solution.py:619
  55.2 8.7 %collective-permute-start.4 = (bf16[640,256]{1,0:T(8,128)(2,1)}, bf16[640,256]{1,0:T(8,128)(2,1)}, u32[]{:S(2)}, u32[]{:S(2)}) collective-permute-start(bf16[640,256]{1,0:T(8,128)(2,1)} %get-tuple-element.41), channel_id=1, source_target_pairs={{0,192},{64,0},{128,64},{192,128},{1,193},{65,1},{129,65},{193,129... | collective-permute-start | bytes 983048 | tf_op jit(solution)/shard_map/ppermute | solution.py:619
  57.0 18.7 %copy-start.14 = (s32[32]{0:T(128)S(1)}, s32[32]{0:T(128)}, u32[]{:S(2)}) copy-start(s32[32]{0:T(128)} %lengths.1) | copy-start | bytes 388
  61.9 13.8 %copy-start.6 = (bf16[32,128,128]{2,1,0:T(8,128)(2,1)S(1)}, bf16[32,128,128]{2,1,0:T(8,128)(2,1)}, u32[]{:S(2)}) copy-start(bf16[32,128,128]{2,1,0:T(8,128)(2,1)} %get-tuple-element.45.qp_ref.q_one) | copy-start | bytes 3145732
  63.9 1.0 copy-start.9
  64.9 10.8 %copy-start = (f32[32,128,128]{2,1,0:T(8,128)S(1)}, f32[32,128,128]{2,1,0:T(8,128)}, u32[]{:S(2)}) copy-start(f32[32,128,128]{2,1,0:T(8,128)} %get-tuple-element.39.refs_1_.lse_ref.lse_one) | copy-start | bytes 6291460
  64.9 10.8 %copy-start.5 = (f32[32,128,128]{2,1,0:T(8,128)S(1)}, f32[32,128,128]{2,1,0:T(8,128)}, u32[]{:S(2)}) copy-start(f32[32,128,128]{2,1,0:T(8,128)} %get-tuple-element.44.old_ref) | copy-start | bytes 6291460
  68.0 3.9 %collective-permute-start.10 = (bf16[128,384]{1,0:T(8,128)(2,1)S(1)}, bf16[128,384]{1,0:T(8,128)(2,1)S(1)}, u32[]{:S(2)}, u32[]{:S(2)}) collective-permute-start(bf16[128,384]{1,0:T(8,128)(2,1)S(1)} %get-tuple-element.52), channel_id=1, source_target_pairs={{0,4},{2,6},{4,0},{6,2},{1,5},{3,7},{5,1},{7,3},{8,12},{10,14},{12... | collective-permute-start | bytes 294920 | tf_op jit(solution)/shard_map/ppermute | solution.py:623
  69.0 6.7 %collective-permute-start.11 = (bf16[128,384]{1,0:T(8,128)(2,1)S(1)}, bf16[128,384]{1,0:T(8,128)(2,1)S(1)}, u32[]{:S(2)}, u32[]{:S(2)}) collective-permute-start(bf16[128,384]{1,0:T(8,128)(2,1)S(1)} %get-tuple-element.51), channel_id=1, source_target_pairs={{0,6},{2,4},{4,2},{6,0},{1,7},{3,5},{5,3},{7,1},{8,14},{10,12},{12... | collective-permute-start | bytes 294920 | tf_op jit(solution)/shard_map/ppermute | solution.py:623
  71.7 4.0 %collective-permute-start.9 = (bf16[128,384]{1,0:T(8,128)(2,1)S(1)}, bf16[128,384]{1,0:T(8,128)(2,1)S(1)}, u32[]{:S(2)}, u32[]{:S(2)}) collective-permute-start(bf16[128,384]{1,0:T(8,128)(2,1)S(1)} %get-tuple-element.53), channel_id=1, source_target_pairs={{0,2},{2,0},{4,6},{6,4},{1,3},{3,1},{5,7},{7,5},{8,10},{10,8},{12,... | collective-permute-start | bytes 294920 | tf_op jit(solution)/shard_map/ppermute | solution.py:623
  82.0 1.1 copy-start.10
  83.1 42.7 %all-to-all-start.3 = ((bf16[32,160,128]{2,1,0:T(8,128)(2,1)}), bf16[32,160,128]{2,1,0:T(8,128)(2,1)S(1)}, u32[]{:S(2)}, u32[]{:S(2)}) async-start(bf16[32,160,128]{2,1,0:T(8,128)(2,1)} %copy-done.10), calls=%async_computation.3 | async-start | bytes 2621440 | tf_op jit(solution)/shard_map/all_to_all | solution.py:629
  92.4 14.7 %collective-permute-start.12 = (bf16[8,128,128]{2,1,0:T(8,128)(2,1)S(1)}, bf16[8,128,128]{2,1,0:T(8,128)(2,1)S(1)}, u32[]{:S(2)}, u32[]{:S(2)}) collective-permute-start(bf16[8,128,128]{2,1,0:T(8,128)(2,1)S(1)} %all-to-all-done.2.refs_9_.e0), channel_id=1, source_target_pairs={{0,64},{64,128},{128,192},{192,0},{1,65},{65,129},{129,193},{193,1... | collective-permute-start | bytes 786440 | tf_op jit(solution)/shard_map/ppermute | solution.py:630
  93.7 23.6 %collective-permute-start.13 = (bf16[8,128,128]{2,1,0:T(8,128)(2,1)S(1)}, bf16[8,128,128]{2,1,0:T(8,128)(2,1)S(1)}, u32[]{:S(2)}, u32[]{:S(2)}) collective-permute-start(bf16[8,128,128]{2,1,0:T(8,128)(2,1)S(1)} %all-to-all-done.2.refs_9_.e0), channel_id=1, source_target_pairs={{0,128},{64,192},{128,0},{192,64},{1,129},{65,193},{129,1},{193,65... | collective-permute-start | bytes 786440 | tf_op jit(solution)/shard_map/ppermute | solution.py:630
  96.1 21.2 %collective-permute-start.14 = (bf16[8,128,128]{2,1,0:T(8,128)(2,1)S(1)}, bf16[8,128,128]{2,1,0:T(8,128)(2,1)S(1)}, u32[]{:S(2)}, u32[]{:S(2)}) collective-permute-start(bf16[8,128,128]{2,1,0:T(8,128)(2,1)S(1)} %all-to-all-done.2.refs_9_.e0), channel_id=1, source_target_pairs={{0,192},{64,0},{128,64},{192,128},{1,193},{65,1},{129,65},{193,129... | collective-permute-start | bytes 786440 | tf_op jit(solution)/shard_map/ppermute | solution.py:630
  97.5 32.2 %copy-start.12 = (bf16[2,4,128,128]{3,1,0,2:T(4,128)(2,1)}, bf16[2,4,128,128]{3,1,0,2:T(4,128)(2,1)S(1)}, u32[]{:S(2)}) copy-start(bf16[2,4,128,128]{3,1,0,2:T(4,128)(2,1)S(1)} %copy.22) | copy-start | bytes 786436
  (2 other events, 1.7 us)

commit v4 on v3

--- a/solution.py
+++ b/solution.py
@@ -34,6 +34,7 @@
 BF16 = jnp.bfloat16
 VMEM_BYTES = 40 * 1024 * 1024
 VMEM_MOST = 60 * 1024 * 1024
+VMEM_LEAST = 16 * 1024 * 1024
 
 
 SMALL = pl.CostEstimate(flops=1000, bytes_accessed=1000, transcendentals=0)
@@ -211,19 +212,21 @@
 
 
 def halves_kernel(before, beyond, _, low, high):
-    half = DEPTH // 2
-    low[...] = before[:half]
-    high[...] = beyond[half:]
+    low[...] = before[...]
+    high[...] = beyond[...]
 
 
 def halves(before, beyond, later):
-    shape = jax.ShapeDtypeStruct((DEPTH // 2, 2 * HEAD), BF16)
+    half = (DEPTH // 2, 2 * HEAD)
+    low, high = pl.BlockSpec(half, lambda i: (0, 0)), pl.BlockSpec(half, lambda i: (1, 0))
+    shape = jax.ShapeDtypeStruct(half, BF16)
     return pl.pallas_call(
         halves_kernel,
-        in_specs=[whole(), whole(), pl.BlockSpec(memory_space=pl.ANY)],
-        out_specs=(whole(),) * 2,
+        grid=(1,),
+        in_specs=[low, high, pl.BlockSpec(memory_space=pl.ANY)],
+        out_specs=(low, low),
         out_shape=(shape,) * 2,
-        compiler_params=params(),
+        compiler_params=params(VMEM_LEAST),
         cost_estimate=SMALL,
         name="halves",
     )(before, beyond, later)
@@ -272,7 +275,7 @@
         + [pl.BlockSpec(memory_space=pl.ANY)] * len(later),
         out_specs=whole(),
         out_shape=jax.ShapeDtypeStruct((sources, TOKENS, width), dtype),
-        compiler_params=params(),
+        compiler_params=params(VMEM_LEAST),
         cost_estimate=SMALL,
         name="project",
     )(me, *weights, *inputs, *carried, *later)

time: 131 us -> 131 us (level)
  transfers between devices with their start and end apart: 18 -> 18, of which waited for: 7 -> 7; matrix products, arithmetic and copies ran while one was open for 2% -> 2% of each run, Pallas kernels for 16% -> 15%
where the time goes in v4:
time: 131 us; the launch traced here: 130 us
  starting transfers between devices  45.1 us (34%)
  waiting for transfers between devices  39 us (30%)
  Pallas kernels  35.1 us (27%)
  local copies, waits for them, and re-layouts  6.51 us (5%)
  other arithmetic  2.16 us (2%)
  between operations  1.68 us (1%)
    ppermute x3, waiting for transfers between devices, on_device(): extras = [extra] + [lax.ppermute(extra, 'y', shift_y(k)) for k in (1, 2, 3)]  19.9 us
    all_to_all x1, starting transfers between devices, on_device(): lax.all_to_all(blocks.reshape(N_Z * N_GEN, ROWS, 2 * HEAD), ('z', 'xl', '...  11.1 us
    all_to_all x1, starting transfers between devices, on_device(): rows = lax.all_to_all(rows, ('y', 'z'), 0, 0, tiled=True)  9.27 us
    pallas_call x1, Pallas kernels, old_attention(): pl.pallas_call(old_kernel, grid_spec=pltpu.PrefetchScalarGridSpec(num_sca...  9.03 us
    pallas_call x3, Pallas kernels, project(): pl.pallas_call(functools.partial(project_kernel, shifts, sources, 0 if to...  8.93 us
    all_to_all x1, waiting for transfers between devices, on_device(): rows = lax.all_to_all(rows, ('y', 'z'), 0, 0, tiled=True)  8.43 us
    pallas_call x1, Pallas kernels, fresh(): pl.pallas_call(fresh_kernel, grid_spec=pltpu.PrefetchScalarGridSpec(num_s...  6.32 us
    unnamed x32, local copies, waits for them, and re-layouts  6.16 us
  transfers between devices with their start and end apart: 18, of which 7 were waited for; matrix products, arithmetic and copies ran while one was open for 2% of the time, Pallas kernels for 15%

profile of v4, /device:TPU:1, one launch (start us, length us, event | category | flops | bytes accessed | tf_op | source)
XLA Modules:
  0.0 129.7 jit_solution(13487243254205948463)
XLA Ops:
  0.6 2.4 %adam.1 = (f32[2,40,512]{2,1,0:T(8,128)}, f32[2,40,512]{2,1,0:T(8,128)}, f32[2,40,512]{2,1,0:T(8,128)}, bf16[8,4,40,256]{3,2,1,0:T(8,128)(2,1)}) custom-call(f32[2,40,512]{2,1,0:T(8,128)} %refs_0_.1, f32[2,40,512]{2,1,0:T(8,128)} %refs_1_.1, f32[2,40,512]{2,1,0:T(8,128)} %refs_2_.1, f32[2,40,512]{2,1,0:T(8,128)} %refs_3_.1), custom_call_target="tpu_custom_call" | custom-call | flops 1000 | bytes 1000 | tf_op jit(solution)/shard_map/adam/pallas_call | solution.py:99
  3.1 11.1 %all-to-all-start.1 = ((bf16[32,40,256]{2,1,0:T(8,128)(2,1)}), bf16[32,40,256]{2,1,0:T(8,128)(2,1)S(1)}, u32[]{:S(2)}, u32[]{:S(2)}) async-start(bf16[32,40,256]{2,1,0:T(8,128)(2,1)} %bitcast.27), calls=%async_computation.1 | async-start | bytes 1310720 | tf_op jit(solution)/shard_map/all_to_all | solution.py:590
  14.1 1.1 copy-done.7
  15.3 2.0 %columns.1 = (bf16[4,128,1280]{2,1,0:T(8,128)(2,1)}, bf16[4,64,1280]{2,1,0:T(8,128)(2,1)}, bf16[4,64,1280]{2,1,0:T(8,128)(2,1)S(1)}) custom-call(bf16[32,4,5120]{2,1,0:T(4,128)(2,1)S(1)} %copy-done.11, bf16[8,4,40,256]{3,2,1,0:T(8,128)(2,1)S(1)} %copy-done.7), custom_call_target="tpu_custom_call" | custom-call | flops 1000 | bytes 1000 | tf_op jit(solution)/shard_map/columns/pallas_call | solution.py:128
  17.5 1.5 %collective-permute-start.5 = (bf16[4,64,1280]{2,1,0:T(8,128)(2,1)}, bf16[4,64,1280]{2,1,0:T(8,128)(2,1)S(1)}, u32[]{:S(2)}, u32[]{:S(2)}) collective-permute-start(bf16[4,64,1280]{2,1,0:T(8,128)(2,1)} %get-tuple-element.42), channel_id=1, source_target_pairs={{0,4},{4,1},{1,5},{5,0},{2,6},{6,3},{3,7},{7,2},{8,12},{12,9},{9,1... | collective-permute-start | bytes 1966088 | tf_op jit(solution)/shard_map/ppermute | solution.py:599
  19.0 1.3 collective-permute-start.6
  20.2 9.0 %old_attention.1 = (f32[32,128,128]{2,1,0:T(8,128)}, f32[32,128,128]{2,1,0:T(8,128)}, bf16[32,128,128]{2,1,0:T(8,128)(2,1)}) custom-call(s32[32]{0:T(128)} %prefix.1, bf16[32,128,128]{2,1,0:T(8,128)(2,1)} %bitcast.34, bf16[32,512,128]{2,1,0:T(8,128)(2,1)} %bitcast.31, bf16[32,512,128]{2,1,0:T(8,128)(2,1)} %bitcast.32, ...), custom_call_target="tpu_custom_call" | custom-call | flops 1000 | bytes 1000 | tf_op jit(solution)/shard_map/old_attention/pallas_call | solution.py:194
  29.3 4.5 %all-to-all-done.1 = bf16[32,40,256]{2,1,0:T(8,128)(2,1)S(1)} async-done(((bf16[32,40,256]{2,1,0:T(8,128)(2,1)}), bf16[32,40,256]{2,1,0:T(8,128)(2,1)S(1)}, u32[]{:S(2)}, u32[]{:S(2)}) %all-to-all-start.1) | async-done | bytes 655392 | tf_op jit(solution)/shard_map/all_to_all | solution.py:590
  34.6 1.3 collective-permute-start
  35.9 1.4 %collective-permute-start.1 = (bf16[1280,256]{1,0:T(8,128)(2,1)}, bf16[1280,256]{1,0:T(8,128)(2,1)}, u32[]{:S(2)}, u32[]{:S(2)}) collective-permute-start(bf16[1280,256]{1,0:T(8,128)(2,1)} %after.2.refs_0_), channel_id=1, source_target_pairs={{0,192},{64,0},{128,64},{192,128},{1,193},{65,1},{129,65},{193,129... | collective-permute-start | bytes 1966088 | tf_op jit(solution)/shard_map/ppermute | solution.py:618
  38.3 1.8 %collective-permute-start.7 = (bf16[4,64,1280]{2,1,0:T(8,128)(2,1)S(1)}, bf16[4,64,1280]{2,1,0:T(8,128)(2,1)}, u32[]{:S(2)}, u32[]{:S(2)}) collective-permute-start(bf16[4,64,1280]{2,1,0:T(8,128)(2,1)S(1)} %collective-permute-done.5.refs_5_.refs_4_), channel_id=1, source_target_pairs={{0,2},{2,0},{1,3},{3,1},{4,6},{6,4},{5,7},{7,5},{8,10},{10,8},{9,1... | collective-permute-start | bytes 1966088 | tf_op jit(solution)/shard_map/ppermute | solution.py:601
  41.9 1.1 copy-done.2
  43.0 1.8 %project.3._.refs_9_ = f32[2,128,256]{2,1,0:T(8,128)S(1)} custom-call(s32[3]{0:T(128)S(1)} %pad_add_fusion.me, bf16[1280,256]{1,0:T(8,128)(2,1)S(1)} %copy-done.2, bf16[4,128,1280]{2,1,0:T(8,128)(2,1)} %get-tuple-element.38._.refs_1_.refs_3_.refs_2_, bf16[4,128,1280]{2,1,0:T(8,128)(2,1)S(1)} %collective-permute-done.2.refs_2_.refs_4_.refs_3_), custom_call_target="tpu_custom_call" | custom-call | flops 1000 | bytes 1000 | tf_op jit(solution)/shard_map/project/pallas_call | solution.py:269
  44.9 1.3 second.1
  46.2 5.3 %all-to-all-start.2 = ((bf16[8,128,128]{2,1,0:T(8,128)(2,1)}), bf16[8,128,128]{2,1,0:T(8,128)(2,1)S(1)}, u32[]{:S(2)}, u32[]{:S(2)}) async-start(bf16[8,128,128]{2,1,0:T(8,128)(2,1)} %second.1), calls=%async_computation.2 | async-start | bytes 524288 | tf_op jit(solution)/shard_map/all_to_all | solution.py:620
  51.7 1.9 %halves.1 = (bf16[640,256]{1,0:T(8,128)(2,1)}, bf16[640,256]{1,0:T(8,128)(2,1)}) custom-call(bf16[1280,256]{1,0:T(8,128)(2,1)} %collective-permute-done.before.refs_1_, bf16[1280,256]{1,0:T(8,128)(2,1)} %collective-permute-done.1.beyond.refs_2_, f32[2,128,256]{2,1,0:T(8,128)S(1)} %project.3._.refs_9_), custom_call_target="tpu_custom_call" | custom-call | flops 1000 | bytes 1000 | tf_op jit(solution)/shard_map/halves/pallas_call | solution.py:223
  53.7 1.3 collective-permute-start.3
  55.0 1.4 %collective-permute-start.4 = (bf16[640,256]{1,0:T(8,128)(2,1)}, bf16[640,256]{1,0:T(8,128)(2,1)}, u32[]{:S(2)}, u32[]{:S(2)}) collective-permute-start(bf16[640,256]{1,0:T(8,128)(2,1)} %get-tuple-element.41), channel_id=1, source_target_pairs={{0,192},{64,0},{128,64},{192,128},{1,193},{65,1},{129,65},{193,129... | collective-permute-start | bytes 983048 | tf_op jit(solution)/shard_map/ppermute | solution.py:622
  56.8 4.1 %project.4.refs_8_ = f32[4,128,256]{2,1,0:T(8,128)S(1)} custom-call(s32[3]{0:T(128)S(1)} %pad_add_fusion.me, bf16[1280,256]{1,0:T(8,128)(2,1)S(1)} %copy-done.3, bf16[1280,256]{1,0:T(8,128)(2,1)} %collective-permute-done.before.refs_1_, bf16[1280,256]{1,0:T(8,128)(2,1)} %collective-permute-done.1.beyond.refs_2_, ...), custom_call_target="tpu_custom_call" | custom-call | flops 1000 | bytes 1000 | tf_op jit(solution)/shard_map/project/pallas_call | solution.py:269
  61.7 2.2 %all-to-all-done.2.refs_9_.e0 = bf16[8,128,128]{2,1,0:T(8,128)(2,1)S(1)} async-done(((bf16[8,128,128]{2,1,0:T(8,128)(2,1)}), bf16[8,128,128]{2,1,0:T(8,128)(2,1)S(1)}, u32[]{:S(2)}, u32[]{:S(2)}) %all-to-all-start.2) | async-done | bytes 262176 | tf_op jit(solution)/shard_map/all_to_all | solution.py:620
  64.9 3.0 %project.5 = bf16[4,128,384]{2,1,0:T(8,128)(2,1)S(1)} custom-call(s32[3]{0:T(128)S(1)} %pad_add_fusion.me, bf16[640,256]{1,0:T(8,128)(2,1)} %collective-permute-done.3.refs_0_, bf16[640,256]{1,0:T(8,128)(2,1)} %collective-permute-done.4.refs_1_, bf16[4,128,1280]{2,1,0:T(8,128)(2,1)} %get-tuple-element.38._.refs_1_.refs_3_.refs_2_, ...), custom_call_target="tpu_custom_call" | custom-call | flops 1000 | bytes 1000 | tf_op jit(solution)/shard_map/project/pallas_call | solution.py:269
  68.8 2.8 %collective-permute-start.11 = (bf16[128,384]{1,0:T(8,128)(2,1)S(1)}, bf16[128,384]{1,0:T(8,128)(2,1)S(1)}, u32[]{:S(2)}, u32[]{:S(2)}) collective-permute-start(bf16[128,384]{1,0:T(8,128)(2,1)S(1)} %get-tuple-element.51), channel_id=1, source_target_pairs={{0,6},{2,4},{4,2},{6,0},{1,7},{3,5},{5,3},{7,1},{8,14},{10,12},{12... | collective-permute-start | bytes 294920 | tf_op jit(solution)/shard_map/ppermute | solution.py:626
  71.7 3.7 %collective-permute-done.11.p3 = bf16[128,384]{1,0:T(8,128)(2,1)S(1)} collective-permute-done((bf16[128,384]{1,0:T(8,128)(2,1)S(1)}, bf16[128,384]{1,0:T(8,128)(2,1)S(1)}, u32[]{:S(2)}, u32[]{:S(2)}) %collective-permute-start.11) | collective-permute-done | bytes 98336 | tf_op jit(solution)/shard_map/ppermute | solution.py:626
  75.5 6.3 %fresh.1 = (bf16[2,4,128,128]{3,2,1,0:T(8,128)(2,1)S(1)}, bf16[32,160,128]{2,1,0:T(8,128)(2,1)S(1)}, bf16[33,128,128]{2,1,0:T(8,128)(2,1)}) custom-call(s32[32]{0:T(128)S(1)} %copy-done.13, s32[32]{0:T(128)S(1)} %convert_reduce_fusion.slot, s32[32]{0:T(128)S(1)} %copy-done.14, s32[3]{0:T(128)S(1)} %pad_add_fusion.me, ...), custom_call_target="tpu_custom_call" | custom-call | flops 1000 | bytes 1000 | tf_op jit(solution)/shard_map/fresh/pallas_call | solution.py:424
  82.9 9.3 %all-to-all-start.3 = ((bf16[32,160,128]{2,1,0:T(8,128)(2,1)}), bf16[32,160,128]{2,1,0:T(8,128)(2,1)S(1)}, u32[]{:S(2)}, u32[]{:S(2)}) async-start(bf16[32,160,128]{2,1,0:T(8,128)(2,1)} %copy-done.10), calls=%async_computation.3 | async-start | bytes 2621440 | tf_op jit(solution)/shard_map/all_to_all | solution.py:632
  92.2 1.3 %collective-permute-start.12 = (bf16[8,128,128]{2,1,0:T(8,128)(2,1)S(1)}, bf16[8,128,128]{2,1,0:T(8,128)(2,1)S(1)}, u32[]{:S(2)}, u32[]{:S(2)}) collective-permute-start(bf16[8,128,128]{2,1,0:T(8,128)(2,1)S(1)} %all-to-all-done.2.refs_9_.e0), channel_id=1, source_target_pairs={{0,64},{64,128},{128,192},{192,0},{1,65},{65,129},{129,193},{193,1... | collective-permute-start | bytes 786440 | tf_op jit(solution)/shard_map/ppermute | solution.py:633
  93.5 2.4 %collective-permute-start.13 = (bf16[8,128,128]{2,1,0:T(8,128)(2,1)S(1)}, bf16[8,128,128]{2,1,0:T(8,128)(2,1)S(1)}, u32[]{:S(2)}, u32[]{:S(2)}) collective-permute-start(bf16[8,128,128]{2,1,0:T(8,128)(2,1)S(1)} %all-to-all-done.2.refs_9_.e0), channel_id=1, source_target_pairs={{0,128},{64,192},{128,0},{192,64},{1,129},{65,193},{129,1},{193,65... | collective-permute-start | bytes 786440 | tf_op jit(solution)/shard_map/ppermute | solution.py:633
  95.9 1.1 collective-permute-start.14
  97.3 9.6 %collective-permute-done.12.e1 = bf16[8,128,128]{2,1,0:T(8,128)(2,1)S(1)} collective-permute-done((bf16[8,128,128]{2,1,0:T(8,128)(2,1)S(1)}, bf16[8,128,128]{2,1,0:T(8,128)(2,1)S(1)}, u32[]{:S(2)}, u32[]{:S(2)}) %collective-permute-start.12) | collective-permute-done | bytes 262176 | tf_op jit(solution)/shard_map/ppermute | solution.py:633
  106.9 10.2 %collective-permute-done.13.e2 = bf16[8,128,128]{2,1,0:T(8,128)(2,1)S(1)} collective-permute-done((bf16[8,128,128]{2,1,0:T(8,128)(2,1)S(1)}, bf16[8,128,128]{2,1,0:T(8,128)(2,1)S(1)}, u32[]{:S(2)}, u32[]{:S(2)}) %collective-permute-start.13) | collective-permute-done | bytes 262176 | tf_op jit(solution)/shard_map/ppermute | solution.py:633
  117.1 8.4 %all-to-all-done.3.in_ref = bf16[32,160,128]{2,1,0:T(8,128)(2,1)S(1)} async-done(((bf16[32,160,128]{2,1,0:T(8,128)(2,1)}), bf16[32,160,128]{2,1,0:T(8,128)(2,1)S(1)}, u32[]{:S(2)}, u32[]{:S(2)}) %all-to-all-start.3) | async-done | bytes 1310752 | tf_op jit(solution)/shard_map/all_to_all | solution.py:632
  125.6 3.3 %join.1 = (bf16[32,2,128,128]{3,2,1,0:T(8,128)(2,1)}, s32[1]{0:T(128)}) custom-call(s32[3]{0:T(128)S(1)} %pad_add_fusion.me, bf16[32,160,128]{2,1,0:T(8,128)(2,1)S(1)} %all-to-all-done.3.in_ref, bf16[8,128,128]{2,1,0:T(8,128)(2,1)S(1)} %all-to-all-done.2.refs_9_.e0, bf16[8,128,128]{2,1,0:T(8,128)(2,1)S(1)} %collective-permute-done.12.e1, ...), custom_call_target="tpu_custom_call" | custom-call | flops 1000 | bytes 1000 | tf_op jit(solution)/shard_map/join/pallas_call | solution.py:519
  (59 shorter events, 8.6 us)
Async XLA Ops:
  0.6 13.5 %copy-start.11 = (bf16[32,4,5120]{2,1,0:T(4,128)(2,1)S(1)}, bf16[32,4,5120]{2,1,0:T(4,128)(2,1)}, u32[]{:S(2)}) copy-start(bf16[32,4,5120]{2,1,0:T(4,128)(2,1)} %x_ref.1) | copy-start | bytes 3932164
  3.1 30.7 %all-to-all-start.1 = ((bf16[32,40,256]{2,1,0:T(8,128)(2,1)}), bf16[32,40,256]{2,1,0:T(8,128)(2,1)S(1)}, u32[]{:S(2)}, u32[]{:S(2)}) async-start(bf16[32,40,256]{2,1,0:T(8,128)(2,1)} %bitcast.27), calls=%async_computation.1 | async-start | bytes 1310720 | tf_op jit(solution)/shard_map/all_to_all | solution.py:590
  14.1 1.1 copy-start.7
  17.2 24.6 %collective-permute-start.2 = (bf16[4,128,1280]{2,1,0:T(8,128)(2,1)}, bf16[4,128,1280]{2,1,0:T(8,128)(2,1)S(1)}, u32[]{:S(2)}, u32[]{:S(2)}) collective-permute-start(bf16[4,128,1280]{2,1,0:T(8,128)(2,1)} %get-tuple-element.38._.refs_1_.refs_3_.refs_2_), channel_id=1, source_target_pairs={{0,2},{2,0},{1,3},{3,1},{4,6},{6,4},{5,7},{7,5},{8,10},{10,8},{9,1... | collective-permute-start | bytes 3932168 | tf_op jit(solution)/shard_map/ppermute | solution.py:598
  17.5 20.8 %collective-permute-start.5 = (bf16[4,64,1280]{2,1,0:T(8,128)(2,1)}, bf16[4,64,1280]{2,1,0:T(8,128)(2,1)S(1)}, u32[]{:S(2)}, u32[]{:S(2)}) collective-permute-start(bf16[4,64,1280]{2,1,0:T(8,128)(2,1)} %get-tuple-element.42), channel_id=1, source_target_pairs={{0,4},{4,1},{1,5},{5,0},{2,6},{6,3},{3,7},{7,2},{8,12},{12,9},{9,1... | collective-permute-start | bytes 1966088 | tf_op jit(solution)/shard_map/ppermute | solution.py:599
  19.0 21.5 %collective-permute-start.6 = (bf16[4,64,1280]{2,1,0:T(8,128)(2,1)S(1)}, bf16[4,64,1280]{2,1,0:T(8,128)(2,1)}, u32[]{:S(2)}, u32[]{:S(2)}) collective-permute-start(bf16[4,64,1280]{2,1,0:T(8,128)(2,1)S(1)} %get-tuple-element.43), channel_id=1, source_target_pairs={{0,5},{4,0},{1,4},{5,1},{2,7},{6,2},{3,6},{7,3},{8,13},{12,8},{9,1... | collective-permute-start | bytes 1966088 | tf_op jit(solution)/shard_map/ppermute | solution.py:600
  29.3 8.1 %copy-start.13 = (s32[32]{0:T(128)S(1)}, s32[32]{0:T(128)}, u32[]{:S(2)}) copy-start(s32[32]{0:T(128)} %dest.1) | copy-start | bytes 388
  34.6 17.1 %collective-permute-start = (bf16[1280,256]{1,0:T(8,128)(2,1)}, bf16[1280,256]{1,0:T(8,128)(2,1)}, u32[]{:S(2)}, u32[]{:S(2)}) collective-permute-start(bf16[1280,256]{1,0:T(8,128)(2,1)} %after.2.refs_0_), channel_id=1, source_target_pairs={{0,64},{64,128},{128,192},{192,0},{1,65},{65,129},{129,193},{193,1... | collective-permute-start | bytes 1966088 | tf_op jit(solution)/shard_map/ppermute | solution.py:617
  35.9 15.8 %collective-permute-start.1 = (bf16[1280,256]{1,0:T(8,128)(2,1)}, bf16[1280,256]{1,0:T(8,128)(2,1)}, u32[]{:S(2)}, u32[]{:S(2)}) collective-permute-start(bf16[1280,256]{1,0:T(8,128)(2,1)} %after.2.refs_0_), channel_id=1, source_target_pairs={{0,192},{64,0},{128,64},{192,128},{1,193},{65,1},{129,65},{193,129... | collective-permute-start | bytes 1966088 | tf_op jit(solution)/shard_map/ppermute | solution.py:618
  38.3 18.4 %collective-permute-start.7 = (bf16[4,64,1280]{2,1,0:T(8,128)(2,1)S(1)}, bf16[4,64,1280]{2,1,0:T(8,128)(2,1)}, u32[]{:S(2)}, u32[]{:S(2)}) collective-permute-start(bf16[4,64,1280]{2,1,0:T(8,128)(2,1)S(1)} %collective-permute-done.5.refs_5_.refs_4_), channel_id=1, source_target_pairs={{0,2},{2,0},{1,3},{3,1},{4,6},{6,4},{5,7},{7,5},{8,10},{10,8},{9,1... | collective-permute-start | bytes 1966088 | tf_op jit(solution)/shard_map/ppermute | solution.py:601
  40.4 16.3 %collective-permute-start.8 = (bf16[4,64,1280]{2,1,0:T(8,128)(2,1)}, bf16[4,64,1280]{2,1,0:T(8,128)(2,1)}, u32[]{:S(2)}, u32[]{:S(2)}) collective-permute-start(bf16[4,64,1280]{2,1,0:T(8,128)(2,1)} %collective-permute-done.6.refs_6_.refs_5_), channel_id=1, source_target_pairs={{0,2},{2,0},{1,3},{3,1},{4,6},{6,4},{5,7},{7,5},{8,10},{10,8},{9,1... | collective-permute-start | bytes 1966088 | tf_op jit(solution)/shard_map/ppermute | solution.py:601
  41.9 1.1 copy-start.2
  43.0 2.0 %copy-start.4 = (f32[32,128,128]{2,1,0:T(8,128)S(1)}, f32[32,128,128]{2,1,0:T(8,128)}, u32[]{:S(2)}) copy-start(f32[32,128,128]{2,1,0:T(8,128)} %get-tuple-element.44.old_ref) | copy-start | bytes 6291460
  44.8 6.7 %copy-start.16 = (s32[32]{0:T(128)S(1)}, s32[32]{0:T(128)}, u32[]{:S(2)}) copy-start(s32[32]{0:T(128)} %prefix.1) | copy-start | bytes 388
  44.9 11.8 %copy-start.3 = (bf16[1280,256]{1,0:T(8,128)(2,1)S(1)}, bf16[1280,256]{1,0:T(8,128)(2,1)}, u32[]{:S(2)}) copy-start(bf16[1280,256]{1,0:T(8,128)(2,1)} %after.2.refs_0_) | copy-start | bytes 1966084
  46.2 17.7 %all-to-all-start.2 = ((bf16[8,128,128]{2,1,0:T(8,128)(2,1)}), bf16[8,128,128]{2,1,0:T(8,128)(2,1)S(1)}, u32[]{:S(2)}, u32[]{:S(2)}) async-start(bf16[8,128,128]{2,1,0:T(8,128)(2,1)} %second.1), calls=%async_computation.2 | async-start | bytes 524288 | tf_op jit(solution)/shard_map/all_to_all | solution.py:620
  53.7 10.2 %collective-permute-start.3 = (bf16[640,256]{1,0:T(8,128)(2,1)}, bf16[640,256]{1,0:T(8,128)(2,1)}, u32[]{:S(2)}, u32[]{:S(2)}) collective-permute-start(bf16[640,256]{1,0:T(8,128)(2,1)} %get-tuple-element.40), channel_id=1, source_target_pairs={{0,64},{64,128},{128,192},{192,0},{1,65},{65,129},{129,193},{193,1... | collective-permute-start | bytes 983048 | tf_op jit(solution)/shard_map/ppermute | solution.py:622
  55.0 8.9 %collective-permute-start.4 = (bf16[640,256]{1,0:T(8,128)(2,1)}, bf16[640,256]{1,0:T(8,128)(2,1)}, u32[]{:S(2)}, u32[]{:S(2)}) collective-permute-start(bf16[640,256]{1,0:T(8,128)(2,1)} %get-tuple-element.41), channel_id=1, source_target_pairs={{0,192},{64,0},{128,64},{192,128},{1,193},{65,1},{129,65},{193,129... | collective-permute-start | bytes 983048 | tf_op jit(solution)/shard_map/ppermute | solution.py:622
  56.8 18.7 %copy-start.14 = (s32[32]{0:T(128)S(1)}, s32[32]{0:T(128)}, u32[]{:S(2)}) copy-start(s32[32]{0:T(128)} %lengths.1) | copy-start | bytes 388
  61.7 13.8 %copy-start.6 = (bf16[32,128,128]{2,1,0:T(8,128)(2,1)S(1)}, bf16[32,128,128]{2,1,0:T(8,128)(2,1)}, u32[]{:S(2)}) copy-start(bf16[32,128,128]{2,1,0:T(8,128)(2,1)} %get-tuple-element.45.qp_ref.q_one) | copy-start | bytes 3145732
  63.9 1.0 copy-start.9
  64.9 10.6 %copy-start = (f32[32,128,128]{2,1,0:T(8,128)S(1)}, f32[32,128,128]{2,1,0:T(8,128)}, u32[]{:S(2)}) copy-start(f32[32,128,128]{2,1,0:T(8,128)} %get-tuple-element.39.refs_1_.lse_ref.lse_one) | copy-start | bytes 6291460
  64.9 10.6 %copy-start.5 = (f32[32,128,128]{2,1,0:T(8,128)S(1)}, f32[32,128,128]{2,1,0:T(8,128)}, u32[]{:S(2)}) copy-start(f32[32,128,128]{2,1,0:T(8,128)} %get-tuple-element.44.old_ref) | copy-start | bytes 6291460
  68.0 3.7 %collective-permute-start.10 = (bf16[128,384]{1,0:T(8,128)(2,1)S(1)}, bf16[128,384]{1,0:T(8,128)(2,1)S(1)}, u32[]{:S(2)}, u32[]{:S(2)}) collective-permute-start(bf16[128,384]{1,0:T(8,128)(2,1)S(1)} %get-tuple-element.52), channel_id=1, source_target_pairs={{0,4},{2,6},{4,0},{6,2},{1,5},{3,7},{5,1},{7,3},{8,12},{10,14},{12... | collective-permute-start | bytes 294920 | tf_op jit(solution)/shard_map/ppermute | solution.py:626
  68.8 6.7 %collective-permute-start.11 = (bf16[128,384]{1,0:T(8,128)(2,1)S(1)}, bf16[128,384]{1,0:T(8,128)(2,1)S(1)}, u32[]{:S(2)}, u32[]{:S(2)}) collective-permute-start(bf16[128,384]{1,0:T(8,128)(2,1)S(1)} %get-tuple-element.51), channel_id=1, source_target_pairs={{0,6},{2,4},{4,2},{6,0},{1,7},{3,5},{5,3},{7,1},{8,14},{10,12},{12... | collective-permute-start | bytes 294920 | tf_op jit(solution)/shard_map/ppermute | solution.py:626
  71.5 4.0 %collective-permute-start.9 = (bf16[128,384]{1,0:T(8,128)(2,1)S(1)}, bf16[128,384]{1,0:T(8,128)(2,1)S(1)}, u32[]{:S(2)}, u32[]{:S(2)}) collective-permute-start(bf16[128,384]{1,0:T(8,128)(2,1)S(1)} %get-tuple-element.53), channel_id=1, source_target_pairs={{0,2},{2,0},{4,6},{6,4},{1,3},{3,1},{5,7},{7,5},{8,10},{10,8},{12,... | collective-permute-start | bytes 294920 | tf_op jit(solution)/shard_map/ppermute | solution.py:626
  81.8 1.1 copy-start.10
  82.9 42.7 %all-to-all-start.3 = ((bf16[32,160,128]{2,1,0:T(8,128)(2,1)}), bf16[32,160,128]{2,1,0:T(8,128)(2,1)S(1)}, u32[]{:S(2)}, u32[]{:S(2)}) async-start(bf16[32,160,128]{2,1,0:T(8,128)(2,1)} %copy-done.10), calls=%async_computation.3 | async-start | bytes 2621440 | tf_op jit(solution)/shard_map/all_to_all | solution.py:632
  92.2 14.7 %collective-permute-start.12 = (bf16[8,128,128]{2,1,0:T(8,128)(2,1)S(1)}, bf16[8,128,128]{2,1,0:T(8,128)(2,1)S(1)}, u32[]{:S(2)}, u32[]{:S(2)}) collective-permute-start(bf16[8,128,128]{2,1,0:T(8,128)(2,1)S(1)} %all-to-all-done.2.refs_9_.e0), channel_id=1, source_target_pairs={{0,64},{64,128},{128,192},{192,0},{1,65},{65,129},{129,193},{193,1... | collective-permute-start | bytes 786440 | tf_op jit(solution)/shard_map/ppermute | solution.py:633
  93.5 23.6 %collective-permute-start.13 = (bf16[8,128,128]{2,1,0:T(8,128)(2,1)S(1)}, bf16[8,128,128]{2,1,0:T(8,128)(2,1)S(1)}, u32[]{:S(2)}, u32[]{:S(2)}) collective-permute-start(bf16[8,128,128]{2,1,0:T(8,128)(2,1)S(1)} %all-to-all-done.2.refs_9_.e0), channel_id=1, source_target_pairs={{0,128},{64,192},{128,0},{192,64},{1,129},{65,193},{129,1},{193,65... | collective-permute-start | bytes 786440 | tf_op jit(solution)/shard_map/ppermute | solution.py:633
  95.9 21.2 %collective-permute-start.14 = (bf16[8,128,128]{2,1,0:T(8,128)(2,1)S(1)}, bf16[8,128,128]{2,1,0:T(8,128)(2,1)S(1)}, u32[]{:S(2)}, u32[]{:S(2)}) collective-permute-start(bf16[8,128,128]{2,1,0:T(8,128)(2,1)S(1)} %all-to-all-done.2.refs_9_.e0), channel_id=1, source_target_pairs={{0,192},{64,0},{128,64},{192,128},{1,193},{65,1},{129,65},{193,129... | collective-permute-start | bytes 786440 | tf_op jit(solution)/shard_map/ppermute | solution.py:633
  97.3 32.2 %copy-start.12 = (bf16[2,4,128,128]{3,1,0,2:T(4,128)(2,1)}, bf16[2,4,128,128]{3,1,0,2:T(4,128)(2,1)S(1)}, u32[]{:S(2)}) copy-start(bf16[2,4,128,128]{3,1,0,2:T(4,128)(2,1)S(1)} %copy.22) | copy-start | bytes 786436
  (2 other events, 1.7 us)
